TPU v7x, 128 devices: a whole 4x4x4 slice. The times are simulated.
128 devices in a mesh: ctx: 2 (over core), dp: 64 (over z, y, x).
Axes of the slice: x: 4, y: 4, z: 4, core: 2. Of those that a mesh axis runs over, the one named last changes fastest.
Arguments:
- query_input: bfloat16 [64, 1024, 3072], P('dp', 'ctx'), may hold values from -6 to 6
- key_input: bfloat16 [64, 1024, 3072], P('dp', 'ctx'), may hold values from -6 to 6
- value_input: bfloat16 [64, 1024, 3072], P('dp', 'ctx'), may hold values from -6 to 6
- out_grad: bfloat16 [64, 1024, 3072], P('dp', 'ctx'), may hold values from -6 to 6
- log_decay: float32 [64, 24, 1024], P('dp', None, 'ctx'), may hold values from -1.5 to 0
- conv_kernel: float32 [3, 4, 3072], replicated, may hold values from -3 to 3
Outputs:
- query_grad: bfloat16 [64, 1024, 3072], P('dp', 'ctx')
- key_grad: bfloat16 [64, 1024, 3072], P('dp', 'ctx')
- value_grad: bfloat16 [64, 1024, 3072], P('dp', 'ctx')
- kernel_grad: float32 [3, 4, 3072], P(None, None, 'dp')
All inputs are finite; a program needn't handle non-finite values.
Results may differ from a plain program's by a relative error of at most 0.0085.
Values may be sent and summed in bfloat16 or wider, within the bound.
A program may use at most 128 MiB of HBM per device.

v0:
```python
import jax
import jax.numpy as jnp
from jax import lax
from jax.sharding import PartitionSpec as P

BLK = 256


def shifted(value, axis, by):
    length = lax.axis_size(axis)
    pairs = [(i, i + by) for i in range(length) if 0 <= i + by < length]
    return lax.ppermute(value, axis, pairs)


def causal_conv(extended, kernel, length):
    rim_rows = kernel.shape[0] - 1
    running = jnp.zeros((length, extended.shape[1]), jnp.float32)
    for offset in range(kernel.shape[0]):
        first_row = rim_rows - offset
        running = running + kernel[offset] * extended[first_row : first_row + length].astype(
            jnp.float32
        )
    return running


def transpose_conv(extended, kernel, length):
    running = jnp.zeros((length, extended.shape[1]), jnp.float32)
    for offset in range(kernel.shape[0]):
        running = running + kernel[offset] * extended[offset : offset + length].astype(jnp.float32)
    return running


def kernel_terms(extended, gradients, length):
    rim_rows = extended.shape[0] - length
    grad_wide = gradients.astype(jnp.float32)
    rows_list = []
    for offset in range(rim_rows + 1):
        first_row = rim_rows - offset
        rows_list.append(
            jnp.sum(
                extended[first_row : first_row + length].astype(jnp.float32) * grad_wide, axis=0
            )
        )
    return jnp.stack(rows_list)


def local(query_input, key_input, value_input, out_grad, log_decay, conv_kernel):
    length = query_input.shape[1]
    inner_width = query_input.shape[2]
    rim_rows = conv_kernel.shape[1] - 1
    head_count = log_decay.shape[1]
    head_size = inner_width // head_count
    blocks = length // BLK
    scores_scale = 1.0 / head_size
    inputs = (query_input[0], key_input[0], value_input[0])
    tail_rows = jnp.stack([source[length - rim_rows :] for source in inputs])
    before = shifted(tail_rows, "ctx", 1)
    extended = [jnp.concatenate([before[member], inputs[member]], axis=0) for member in range(3)]
    convolved = [
        causal_conv(extended[member], conv_kernel[member], length).astype(jnp.bfloat16)
        for member in range(3)
    ]
    block_shape = (blocks, BLK, head_count, head_size)
    query_rows = convolved[0].reshape(block_shape)
    rows_of_keys = convolved[1].reshape(block_shape)
    rows_of_values = convolved[2].reshape(block_shape)
    gradient_rows = out_grad[0].reshape(block_shape)
    local_sum = jnp.cumsum(log_decay[0].reshape(head_count, blocks, BLK), axis=2).transpose(1, 0, 2)
    totals = local_sum[:, :, -1]
    decays = jnp.exp(totals)
    key_matrix = jnp.exp(totals[:, :, None] - local_sum).transpose(0, 2, 1)[..., None]
    query_matrix = jnp.exp(local_sum).transpose(0, 2, 1)[..., None]
    weighted_keys = (rows_of_keys.astype(jnp.float32) * key_matrix).astype(jnp.bfloat16)
    weighted_queries = (query_rows.astype(jnp.float32) * query_matrix).astype(jnp.bfloat16)
    block_states = jnp.einsum(
        "nshk,nshv->nhkv", weighted_keys, rows_of_values, preferred_element_type=jnp.float32
    )
    block_future = jnp.einsum(
        "nthk,nthv->nhkv", weighted_queries, gradient_rows, preferred_element_type=jnp.float32
    )
    zero_state = jnp.zeros((head_count, head_size, head_size), jnp.float32)
    running = zero_state
    decay_run = jnp.ones((head_count,), jnp.float32)
    local_in = []
    decay_before = []
    for block_index in range(blocks):
        local_in.append(running)
        decay_before.append(decay_run)
        running = decays[block_index][:, None, None] * running + block_states[block_index]
        decay_run = decay_run * decays[block_index]
    device_state = running
    device_decay = decay_run
    running = zero_state
    decay_run = jnp.ones((head_count,), jnp.float32)
    local_future = [zero_state] * blocks
    decay_after = [decay_run] * blocks
    for block_index in reversed(range(blocks)):
        local_future[block_index] = running
        decay_after[block_index] = decay_run
        running = block_future[block_index] + decays[block_index][:, None, None] * running
        decay_run = decay_run * decays[block_index]
    device_future = running

    def chain_step(step_index, carried_state):
        state_now, future_now = carried_state
        state_out = device_decay[:, None, None] * state_now + device_state
        future_out = device_future + device_decay[:, None, None] * future_now
        return (
            shifted(state_out.astype(jnp.bfloat16), "ctx", 1).astype(state_out.dtype),
            shifted(future_out.astype(jnp.bfloat16), "ctx", -1).astype(future_out.dtype),
        )

    state_in, grad_in = lax.fori_loop(
        0, lax.axis_size("ctx") - 1, chain_step, (zero_state, zero_state)
    )
    incoming = (jnp.stack(decay_before)[:, :, None, None] * state_in + jnp.stack(local_in)).astype(
        jnp.bfloat16
    )
    future_grads = (
        jnp.stack(decay_after)[:, :, None, None] * grad_in + jnp.stack(local_future)
    ).astype(jnp.bfloat16)
    causal = lax.broadcasted_iota(jnp.int32, (BLK, BLK), 0) >= lax.broadcasted_iota(
        jnp.int32, (BLK, BLK), 1
    )
    differ = local_sum[:, :, :, None] - local_sum[:, :, None, :]
    mask_weight = jnp.where(causal, jnp.exp(jnp.where(causal, differ, 0.0)), 0.0)
    probabilities = (
        jnp.einsum("nthk,nshk->nhts", query_rows, rows_of_keys, preferred_element_type=jnp.float32)
        * scores_scale
        * mask_weight
    ).astype(jnp.bfloat16)
    probability_grads = (
        jnp.einsum(
            "nthv,nshv->nhts", gradient_rows, rows_of_values, preferred_element_type=jnp.float32
        )
        * scores_scale
        * mask_weight
    ).astype(jnp.bfloat16)
    query_change = jnp.einsum(
        "nhts,nshk->nthk", probability_grads, rows_of_keys, preferred_element_type=jnp.float32
    ) + scores_scale * query_matrix * jnp.einsum(
        "nthv,nhkv->nthk", gradient_rows, incoming, preferred_element_type=jnp.float32
    )
    key_change = jnp.einsum(
        "nhts,nthk->nshk", probability_grads, query_rows, preferred_element_type=jnp.float32
    ) + scores_scale * key_matrix * jnp.einsum(
        "nshv,nhkv->nshk", rows_of_values, future_grads, preferred_element_type=jnp.float32
    )
    value_change = jnp.einsum(
        "nhts,nthv->nshv", probabilities, gradient_rows, preferred_element_type=jnp.float32
    ) + scores_scale * key_matrix * jnp.einsum(
        "nshk,nhkv->nshv", rows_of_keys, future_grads, preferred_element_type=jnp.float32
    )
    deltas = [
        member_delta.astype(jnp.bfloat16).reshape(length, inner_width)
        for member_delta in (query_change, key_change, value_change)
    ]
    head_rows = jnp.stack([delta_rows[:rim_rows] for delta_rows in deltas])
    after = shifted(head_rows, "ctx", -1)
    outputs = []
    kernel_part = []
    for member in range(3):
        grown = jnp.concatenate([deltas[member], after[member]], axis=0)
        outputs.append(
            transpose_conv(grown, conv_kernel[member], length).astype(jnp.bfloat16)[None]
        )
        kernel_part.append(kernel_terms(extended[member], deltas[member], length))
    kernel_sums = jnp.stack(kernel_part)
    share_width = inner_width // lax.axis_size("dp")
    summed = lax.psum(kernel_sums, ("ctx", "dp"))
    own_piece = lax.dynamic_slice_in_dim(summed, lax.axis_index("dp") * share_width, share_width, 2)
    kernel_out = own_piece / lax.axis_size("dp")
    return (outputs[0], outputs[1], outputs[2], kernel_out)


def solution(mesh):
    in_specs = (
        P("dp", "ctx", None),
        P("dp", "ctx", None),
        P("dp", "ctx", None),
        P("dp", "ctx", None),
        P("dp", None, "ctx"),
        P(),
    )
    out_specs = (
        P("dp", "ctx", None),
        P("dp", "ctx", None),
        P("dp", "ctx", None),
        P(None, None, "dp"),
    )
    return jax.shard_map(local, mesh=mesh, in_specs=in_specs, out_specs=out_specs, check_vma=False)
```

profile of v0, /device:TPU:1, one launch (start us, length us, event | category | flops | bytes accessed | tf_op | source)
XLA Modules:
  0.0 295.2 jit_solution(413552993413061115)
XLA Ops:
  7.2 0.8 slice.215
  8.0 0.8 slice.216
  10.4 1.3 collective-permute-start
  11.6 0.8 reshape.92
  12.5 1.2 reduce-window.6
  15.4 1.9 fusion.99
  18.0 4.6 %copy.95 = bf16[64,8,24,128]{3,2,1,0:T(8,128)(2,1)} copy(bf16[64,8,24,128]{3,1,2,0:T(8,128)(2,1)} %bitcast.244) | data formatting | bytes 6291456
  23.2 1.4 slice_bitcast_fusion.9
  24.6 3.3 %fusion.67 = bf16[64,8,24,128]{3,1,2,0:T(8,128)(2,1)S(1)} fusion(bf16[512,3072]{1,0:T(8,128)(2,1)S(1)} %bitcast.220, bf16[3,3072]{1,0:T(4,128)(2,1)S(1)} %get-tuple-element.54, f32[3072]{0:T(1024)S(1)} %bitcast.245, f32[3072]{0:T(1024)S(1)} %bitcast.247, f32[3072]{0:T(1024)S(1)} %bitcast.249, f32[3072]{0:T(1024)S(1)} %bitcast.251), kind=kLoop, calls=%fused_computation.113 | loop fusion | flops 33030144 | bytes 6359040
  27.9 2.5 copy.93
  30.4 3.8 %copy.67 = bf16[2,256,24,128]{1,3,2,0:T(8,128)(2,1)S(1)} copy(bf16[2,256,24,128]{3,2,1,0:T(8,128)(2,1)} %bitcast.242) | data formatting | bytes 6291456 | tf_op jit(solution)/shard_map/reshape | solution.py:65
  34.3 7.4 %fusion.66 = bf16[64,8,24,128]{3,1,2,0:T(8,128)(2,1)S(1)} fusion(bf16[512,3072]{1,0:T(8,128)(2,1)} %bitcast.218, bf16[3,3072]{1,0:T(4,128)(2,1)S(1)} %get-tuple-element.52, f32[3072]{0:T(1024)S(1)} %bitcast.255, f32[3072]{0:T(1024)S(1)} %bitcast.257, f32[3072]{0:T(1024)S(1)} %bitcast.259, f32[3072]{0:T(1024)S(1)} %bitcast.253), kind=kLoop, calls=%fused_computation.112 | loop fusion | flops 33030144 | bytes 6359040
  41.6 0.9 copy.94
  42.5 1.1 fusion.63
  43.6 1.3 slice_add_fusion.1
  45.4 1.5 collective-permute-start.1
  46.9 4.8 %fusion = bf16[2,24,256,256]{2,3,1,0:T(8,128)(2,1)S(1)} fusion(f32[2,24,256]{2,1,0:T(8,128)S(1)} %bitcast_bitcast_fusion.1, pred[256,256]{0,1:T(8,128)(4,1)S(1)} %copy-done.22, bf16[2,256,24,128]{3,2,1,0:T(8,128)(2,1)S(1)} %bitcast.233, bf16[2,256,24,128]{3,2,1,0:T(8,128)(2,1)S(1)} %bitcast.230), kind=kOutput, calls=%fused_computation.1 | convolution fusion | flops 824180736 | bytes 12697600 | tf_op jit(solution)/shard_map/nthv,nshv->nhts/dot_general | solution.py:133
  51.8 1.0 fusion.101
  52.8 1.6 copy-done
  54.6 1.2 copy-done.17
  55.8 2.9 fusion.43
  58.8 4.9 %copy.72 = bf16[2,256,24,128]{3,2,1,0:T(8,128)(2,1)} copy(bf16[2,256,24,128]{1,3,2,0:T(8,128)(2,1)} %fusion.43) | data formatting | bytes 6291456 | tf_op jit(solution)/shard_map/convert_element_type | solution.py:155
  63.6 4.5 %copy.149 = bf16[64,8,24,128]{3,1,2,0:T(8,128)(2,1)} copy(bf16[64,8,24,128]{3,2,1,0:T(8,128)(2,1)} %bitcast.222) | data formatting | bytes 6291456
  68.2 6.2 %fusion.18 = (f32[3072]{0:T(1024)S(1)}, f32[3072]{0:T(1024)S(1)}, f32[3072]{0:T(1024)S(1)}, f32[3072]{0:T(1024)}, bf16[64,8,24,128]{3,1,2,0:T(8,128)(2,1)S(1)}) fusion(bf16[512,3072]{1,0:T(8,128)(2,1)S(1)} %bitcast.241, bf16[3,3072]{1,0:T(4,128)(2,1)S(1)} %copy-done.21, bf16[64,8,24,128]{3,2,1,0:T(8,128)(2,1)S(1)} %bitcast.223, ...), kind=kLoop, calls=%fused_computation.48 | loop fusion | flops 61329408 | bytes 12699648 | tf_op jit(solution)/shard_map/reduce_sum | solution.py:40
  74.4 2.5 copy.97
  77.0 4.9 %copy.73 = bf16[2,256,24,128]{1,3,2,0:T(8,128)(2,1)} copy(bf16[2,256,24,128]{3,2,1,0:T(8,128)(2,1)} %bitcast.243) | data formatting | bytes 6291456 | tf_op jit(solution)/shard_map/reshape | solution.py:64
  81.8 9.6 %fusion.21 = f32[2,24,256,128]{2,3,1,0:T(8,128)} fusion(f32[2,24,256]{2,1,0:T(8,128)S(1)} %bitcast_bitcast_fusion.1, pred[256,256]{0,1:T(8,128)(4,1)} %iota_compare_fusion, bf16[2,256,24,128]{1,3,2,0:T(8,128)(2,1)} %copy.73, bf16[2,256,24,128]{1,3,2,0:T(8,128)(2,1)S(1)} %copy.67, bf16[2,256,24,128]{3,2,1,0:T(8,128)(2,1)} %bitcast.228), kind=kOutput, calls=%fused_computation.51 | convolution fusion | flops 1629487104 | bytes 15843328 | tf_op jit(solution)/shard_map/nhts,nthv->nshv/dot_general | solution.py:149
  91.4 4.1 %fusion.64 = f32[2,24,128,128]{3,2,1,0:T(8,128)S(1)} fusion(bf16[2,256,24,128]{1,3,2,0:T(8,128)(2,1)} %copy.73, f32[2,256,24]{1,2,0:T(8,128)S(1)} %get-tuple-element.56, bf16[2,256,24,128]{3,2,1,0:T(8,128)(2,1)} %bitcast.229), kind=kOutput, calls=%fused_computation.110 | convolution fusion | flops 407371776 | bytes 9486336 | tf_op jit(solution)/shard_map/nthk,nthv->nhkv/dot_general | solution.py:78
  95.7 1.3 fusion.82
  97.0 5.0 %collective-permute-start.2 = (bf16[24,128,128]{2,1,0:T(8,128)(2,1)}, bf16[24,128,128]{2,1,0:T(8,128)(2,1)}, u32[]{:S(2)}, u32[]{:S(2)}) collective-permute-start(bf16[24,128,128]{2,1,0:T(8,128)(2,1)} %fusion.82), channel_id=1, source_target_pairs={{64,0},{65,1},{66,2},{67,3},{68,4},{69,5},{70,6},{71,7},{72,8},{73... | collective-permute-start | bytes 2359304 | tf_op jit(solution)/shard_map/while/body/eval_jaxpr/ppermute | solution.py:12
  103.0 2.2 fusion.102
  105.2 1.3 convert_element_type.180
  106.5 1.2 copy-done.1
  107.6 3.0 %fusion.41 = bf16[2,256,24,128]{1,3,2,0:T(8,128)(2,1)} fusion(f32[2,24,128,256]{3,2,1,0:T(8,128)S(1)} %fusion.102, f32[2,256,24]{1,2,0:T(8,128)S(1)} %get-tuple-element.57, bf16[2,256,24,128]{3,2,1,0:T(8,128)(2,1)S(1)} %bitcast.234, f32[1,24,128,128]{3,2,1,0:T(8,128)S(1)} %slice_add_fusion, f32[24,128,128]{2,1,0:T(8,128)S(1)} %convert_element_type.180, ...), kind=kOutput, calls=%fused_computation.73 | convolution fusion | flops 409731072 | bytes 15777984 | tf_op jit(solution)/shard_map/nshv,nhkv->nshk/dot_general | solution.py:146
  110.6 4.8 %copy.78 = bf16[2,256,24,128]{3,2,1,0:T(8,128)(2,1)} copy(bf16[2,256,24,128]{1,3,2,0:T(8,128)(2,1)} %fusion.41) | data formatting | bytes 6291456 | tf_op jit(solution)/shard_map/convert_element_type | solution.py:155
  115.4 6.7 %fusion.39 = bf16[2,256,24,128]{1,3,2,0:T(8,128)(2,1)} fusion(f32[2,24,256,128]{2,3,1,0:T(8,128)} %fusion.21, f32[2,256,24]{1,2,0:T(8,128)S(1)} %get-tuple-element.57, bf16[2,256,24,128]{1,3,2,0:T(8,128)(2,1)S(1)} %copy.67, f32[1,24,128,128]{3,2,1,0:T(8,128)} %copy-done.12, f32[24,128,128]{2,1,0:T(8,128)} %copy-done.1, f32[2,24]{1,0:T(2,128)S(1)} %stack.93), kind=kOutput, calls=%fused_computation.70 | convolution fusion | flops 409731072 | bytes 15777984 | tf_op jit(solution)/shard_map/nshk,nhkv->nshv/dot_general | solution.py:151
  122.1 5.0 %copy.86 = bf16[2,256,24,128]{3,2,1,0:T(8,128)(2,1)} copy(bf16[2,256,24,128]{1,3,2,0:T(8,128)(2,1)} %fusion.39) | data formatting | bytes 6291456 | tf_op jit(solution)/shard_map/convert_element_type | solution.py:155
  127.1 0.9 copy.148
  128.0 1.1 copy-done.2
  129.1 2.0 copy-done.4
  131.1 9.0 %fusion.27 = (f32[3072]{0:T(1024)S(1)}, f32[3072]{0:T(1024)S(1)}, f32[3072]{0:T(1024)S(1)}, f32[3072]{0:T(1024)S(1)}, f32[3072]{0:T(1024)S(1)}, /*index=5*/f32[3072]{0:T(1024)S(1)}, f32[3072]{0:T(1024)S(1)}, f32[3072]{0:T(1024)S(1)}) fusion(bf16[512,3072]{1,0:T(8,128)(2,1)S(1)} %bitcast.221, bf16[3,3072]{1,0:T(4,128)(2,1)S(1)} %get-tuple-element.54, ...), kind=kLoop, calls=%fused_computation.57 | loop fusion | flops 69181440 | bytes 19009536 | tf_op jit(solution)/shard_map/reduce_sum | solution.py:40
  140.1 0.9 copy.147
  141.7 1.9 collective-permute-start.3
  145.3 4.6 %fusion.70 = bf16[1,512,3072]{2,1,0:T(8,128)(2,1)} fusion(bf16[3,3072]{1,0:T(4,128)(2,1)S(1)} %get-tuple-element.49, bf16[512,3072]{1,0:T(8,128)(2,1)S(1)} %bitcast.240, f32[3072]{0:T(1024)S(1)} %bitcast.256, f32[3072]{0:T(1024)S(1)} %bitcast.258, f32[3072]{0:T(1024)S(1)} %bitcast.260, f32[3072]{0:T(1024)S(1)} %bitcast.254), kind=kLoop, calls=%fused_computation.127 | loop fusion | flops 33030144 | bytes 6359040 | tf_op jit(solution)/shard_map/broadcast_in_dim | solution.py:165
  149.9 4.6 %fusion.71 = bf16[1,512,3072]{2,1,0:T(8,128)(2,1)} fusion(bf16[3,3072]{1,0:T(4,128)(2,1)S(1)} %get-tuple-element.50, bf16[512,3072]{1,0:T(8,128)(2,1)S(1)} %bitcast.238, f32[3072]{0:T(1024)S(1)} %bitcast.246, f32[3072]{0:T(1024)S(1)} %bitcast.248, f32[3072]{0:T(1024)S(1)} %bitcast.250, f32[3072]{0:T(1024)S(1)} %bitcast.252), kind=kLoop, calls=%fused_computation.128 | loop fusion | flops 33030144 | bytes 6359040 | tf_op jit(solution)/shard_map/broadcast_in_dim | solution.py:165
  154.5 4.6 %fusion.72 = bf16[1,512,3072]{2,1,0:T(8,128)(2,1)} fusion(bf16[3,3072]{1,0:T(4,128)(2,1)S(1)} %get-tuple-element.51, bf16[512,3072]{1,0:T(8,128)(2,1)S(1)} %bitcast.236, f32[3072]{0:T(1024)S(1)} %bitcast.266, f32[3072]{0:T(1024)S(1)} %bitcast.268, f32[3072]{0:T(1024)S(1)} %bitcast.262, f32[3072]{0:T(1024)S(1)} %bitcast.264), kind=kLoop, calls=%fused_computation.129 | loop fusion | flops 33030144 | bytes 6359040 | tf_op jit(solution)/shard_map/broadcast_in_dim | solution.py:165
  159.1 128.0 %all-reduce.6.cloned.1.call-done = f32[3,4,3072]{2,1,0:T(4,128)} async-done(((f32[3,4,3072]{2,1,0:T(4,128)}), f32[3,4,3072]{2,1,0:T(4,128)}) %all-reduce.6.cloned.1.call-update) | async-done | bytes 147472 | tf_op jit(solution)/shard_map/psum | solution.py:170
  287.0 1.4 dynamic-slice_multiply_fusion
  (96 shorter events, 8.6 us)
Async XLA Ops:
  7.2 279.9 %all-reduce.6.cloned.1.call-start = ((), (), s32[]{:S(2)}) async-start(), calls=%async_computation | async-start | bytes 294912 | tf_op jit(solution)/shard_map/psum | solution.py:170
  10.4 12.8 %collective-permute-start = (bf16[3,3,3072]{2,1,0:T(4,128)(2,1)}, bf16[3,3,3072]{2,1,0:T(4,128)(2,1)}, u32[]{:S(2)}, u32[]{:S(2)}) collective-permute-start(bf16[3,3,3072]{2,1,0:T(4,128)(2,1)} %pad_maximum_fusion.7), channel_id=1, source_target_pairs={{0,64},{1,65},{2,66},{3,67},{4,68},{5,69},{6,70},{7,71},{8,72},{9,... | collective-permute-start | bytes 165896 | tf_op jit(solution)/shard_map/ppermute | solution.py:12
  18.0 6.5 %copy-start.3 = (bf16[1,512,3072]{2,1,0:T(8,128)(2,1)S(1)}, bf16[1,512,3072]{2,1,0:T(8,128)(2,1)}, u32[]{:S(2)}) copy-start(bf16[1,512,3072]{2,1,0:T(8,128)(2,1)} %param.7) | copy-start | bytes 9437188
  42.5 4.4 %copy-start.9 = (bf16[64,8,24,128]{3,2,1,0:T(8,128)(2,1)}, bf16[64,8,24,128]{3,2,1,0:T(8,128)(2,1)S(1)}, u32[]{:S(2)}) copy-start(bf16[64,8,24,128]{3,2,1,0:T(8,128)(2,1)S(1)} %copy.94) | copy-start | bytes 9437188
  42.5 1.1 copy-start.28
  42.5 2.4 copy-start.25
  42.5 2.4 copy-start.30
  43.6 3.3 %copy-start.8 = (bf16[64,8,24,128]{3,2,1,0:T(8,128)(2,1)S(1)}, bf16[64,8,24,128]{3,2,1,0:T(8,128)(2,1)}, u32[]{:S(2)}) copy-start(bf16[64,8,24,128]{3,2,1,0:T(8,128)(2,1)} %copy.95) | copy-start | bytes 9437188
  43.6 3.3 %copy-start.22 = (pred[256,256]{0,1:T(8,128)(4,1)S(1)}, pred[256,256]{0,1:T(8,128)(4,1)}, u32[]{:S(2)}) copy-start(pred[256,256]{0,1:T(8,128)(4,1)} %iota_compare_fusion) | copy-start | bytes 196612
  45.4 9.0 %collective-permute-start.1 = (bf16[24,128,128]{2,1,0:T(8,128)(2,1)S(1)}, bf16[24,128,128]{2,1,0:T(8,128)(2,1)S(1)}, u32[]{:S(2)}, u32[]{:S(2)}) collective-permute-start(bf16[24,128,128]{2,1,0:T(8,128)(2,1)S(1)} %fusion.85), channel_id=1, source_target_pairs={{0,64},{1,65},{2,66},{3,67},{4,68},{5,69},{6,70},{7,71},{8,72},{9,... | collective-permute-start | bytes 2359304 | tf_op jit(solution)/shard_map/while/body/eval_jaxpr/ppermute | solution.py:12
  51.8 2.6 copy-start
  51.8 2.8 copy-start.24
  54.4 1.4 copy-start.17
  58.8 9.4 %copy-start.19 = (f32[1,1,3072]{2,1,0:T(1,128)S(1)}, f32[1,1,3072]{2,1,0:T(1,128)}, u32[]{:S(2)}) copy-start(f32[1,1,3072]{2,1,0:T(1,128)} %get-tuple-element.47) | copy-start | bytes 36868
  58.8 9.4 %copy-start.20 = (f32[1,1,3072]{2,1,0:T(1,128)S(1)}, f32[1,1,3072]{2,1,0:T(1,128)}, u32[]{:S(2)}) copy-start(f32[1,1,3072]{2,1,0:T(1,128)} %get-tuple-element.48) | copy-start | bytes 36868
  58.8 9.4 %copy-start.21 = (bf16[3,3072]{1,0:T(4,128)(2,1)S(1)}, bf16[3,3072]{1,0:T(4,128)(2,1)}, u32[]{:S(2)}) copy-start(bf16[3,3072]{1,0:T(4,128)(2,1)} %get-tuple-element.53) | copy-start | bytes 55300
  63.6 4.6 %copy-start.5 = (bf16[2,256,24,128]{3,2,1,0:T(8,128)(2,1)S(1)}, bf16[2,256,24,128]{3,2,1,0:T(8,128)(2,1)}, u32[]{:S(2)}) copy-start(bf16[2,256,24,128]{3,2,1,0:T(8,128)(2,1)} %copy.72) | copy-start | bytes 9437188
  63.6 4.6 %copy-start.16 = (bf16[1,512,3072]{2,1,0:T(8,128)(2,1)S(1)}, bf16[1,512,3072]{2,1,0:T(8,128)(2,1)}, u32[]{:S(2)}) copy-start(bf16[1,512,3072]{2,1,0:T(8,128)(2,1)} %param.6) | copy-start | bytes 9437188
  63.6 4.6 %copy-start.18 = (f32[1,1,3072]{2,1,0:T(1,128)S(1)}, f32[1,1,3072]{2,1,0:T(1,128)}, u32[]{:S(2)}) copy-start(f32[1,1,3072]{2,1,0:T(1,128)} %get-tuple-element.46) | copy-start | bytes 36868
  91.4 11.5 %slice-start = ((s8[6291456]{0:T(1024)(128)(4,1)}), s8[4194304]{0:T(1024)(128)(4,1)S(1)}, s32[]{:S(2)}) async-start(s8[6291456]{0:T(1024)(128)(4,1)} %bitcast.216), calls=%async_computation.1 | async-start | bytes 8388608
  91.4 4.1 %copy-start.27 = (f32[24]{0:T(128)S(1)}, f32[24]{0:T(128)}, u32[]{:S(2)}) copy-start(f32[24]{0:T(128)} %get-tuple-element.64) | copy-start | bytes 292
  91.4 4.3 %copy-start.26 = (f32[24]{0:T(128)S(1)}, f32[24]{0:T(128)}, u32[]{:S(2)}) copy-start(f32[24]{0:T(128)} %get-tuple-element.65) | copy-start | bytes 292
  91.4 4.3 %copy-start.29 = (f32[24]{0:T(128)S(1)}, f32[24]{0:T(128)}, u32[]{:S(2)}) copy-start(f32[24]{0:T(128)} %get-tuple-element.60) | copy-start | bytes 292
  91.4 11.5 %slice-start.1 = ((s8[6291456]{0:T(1024)(128)(4,1)}), s8[2097152]{0:T(1024)(128)(4,1)S(1)}, s32[]{:S(2)}) async-start(s8[6291456]{0:T(1024)(128)(4,1)} %bitcast.216), calls=%async_computation.2 | async-start | bytes 4194304
  95.5 7.4 %copy-start.23 = (f32[3072]{0:T(1024)S(1)}, f32[3072]{0:T(1024)}, u32[]{:S(2)}) copy-start(f32[3072]{0:T(1024)} %get-tuple-element.31) | copy-start | bytes 36868
  95.5 7.5 %copy-start.11 = (bf16[2,256,24,128]{1,3,2,0:T(8,128)(2,1)S(1)}, bf16[2,256,24,128]{1,3,2,0:T(8,128)(2,1)}, u32[]{:S(2)}) copy-start(bf16[2,256,24,128]{1,3,2,0:T(8,128)(2,1)} %copy.73) | copy-start | bytes 9437188
  95.7 10.8 %copy-start.12 = (f32[1,24,128,128]{3,2,1,0:T(8,128)}, f32[1,24,128,128]{3,2,1,0:T(8,128)S(1)}, u32[]{:S(2)}) copy-start(f32[1,24,128,128]{3,2,1,0:T(8,128)S(1)} %slice_add_fusion) | copy-start | bytes 4718596
  97.0 8.1 %collective-permute-start.2 = (bf16[24,128,128]{2,1,0:T(8,128)(2,1)}, bf16[24,128,128]{2,1,0:T(8,128)(2,1)}, u32[]{:S(2)}, u32[]{:S(2)}) collective-permute-start(bf16[24,128,128]{2,1,0:T(8,128)(2,1)} %fusion.82), channel_id=1, source_target_pairs={{64,0},{65,1},{66,2},{67,3},{68,4},{69,5},{70,6},{71,7},{72,8},{73... | collective-permute-start | bytes 2359304 | tf_op jit(solution)/shard_map/while/body/eval_jaxpr/ppermute | solution.py:12
  103.0 4.7 %copy-start.10 = (bf16[64,8,24,128]{3,2,1,0:T(8,128)(2,1)S(1)}, bf16[64,8,24,128]{3,2,1,0:T(8,128)(2,1)}, u32[]{:S(2)}) copy-start(bf16[64,8,24,128]{3,2,1,0:T(8,128)(2,1)} %copy-done.9) | copy-start | bytes 9437188
  106.5 1.2 copy-start.1
  122.1 5.0 %copy-start.6 = (bf16[2,256,24,128]{3,2,1,0:T(8,128)(2,1)S(1)}, bf16[2,256,24,128]{3,2,1,0:T(8,128)(2,1)}, u32[]{:S(2)}) copy-start(bf16[2,256,24,128]{3,2,1,0:T(8,128)(2,1)} %copy.78) | copy-start | bytes 9437188
  127.1 2.0 copy-start.2
  127.1 4.0 %copy-start.4 = (bf16[1,512,3072]{2,1,0:T(8,128)(2,1)S(1)}, bf16[1,512,3072]{2,1,0:T(8,128)(2,1)}, u32[]{:S(2)}) copy-start(bf16[1,512,3072]{2,1,0:T(8,128)(2,1)} %param.7) | copy-start | bytes 9437188
  128.0 13.0 %copy-start.14 = (bf16[64,8,24,128]{3,1,2,0:T(8,128)(2,1)}, bf16[64,8,24,128]{3,1,2,0:T(8,128)(2,1)S(1)}, u32[]{:S(2)}) copy-start(bf16[64,8,24,128]{3,1,2,0:T(8,128)(2,1)S(1)} %copy.148) | copy-start | bytes 9437188
  131.1 9.0 %copy-start.7 = (bf16[2,256,24,128]{3,2,1,0:T(8,128)(2,1)S(1)}, bf16[2,256,24,128]{3,2,1,0:T(8,128)(2,1)}, u32[]{:S(2)}) copy-start(bf16[2,256,24,128]{3,2,1,0:T(8,128)(2,1)} %copy.86) | copy-start | bytes 9437188
  141.7 2.8 collective-permute-start.3
  145.3 4.6 %copy-start.15 = (bf16[64,8,24,128]{3,1,2,0:T(8,128)(2,1)S(1)}, bf16[64,8,24,128]{3,1,2,0:T(8,128)(2,1)}, u32[]{:S(2)}) copy-start(bf16[64,8,24,128]{3,1,2,0:T(8,128)(2,1)} %copy-done.14) | copy-start | bytes 9437188
  149.9 4.6 %copy-start.13 = (bf16[64,8,24,128]{3,1,2,0:T(8,128)(2,1)S(1)}, bf16[64,8,24,128]{3,1,2,0:T(8,128)(2,1)}, u32[]{:S(2)}) copy-start(bf16[64,8,24,128]{3,1,2,0:T(8,128)(2,1)} %copy.149) | copy-start | bytes 9437188
Sparse Core Ops, SparseCore 0:
  144.6 142.4 all-reduce.5
where the time goes:
time: 296 us; the launch traced here: 295 us
  waiting for transfers between devices  128 us (43%)
  local copies, waits for them, and re-layouts  57.1 us (19%)
  other arithmetic  50.6 us (17%)
  matrix products  35.3 us (12%)
  between operations  14.6 us (5%)
  starting transfers between devices  9.75 us (3%)
    psum x1, waiting for transfers between devices, local(): summed = lax.psum(kernel_sums, ('ctx', 'dp'))  128 us
    unnamed x73, local copies, waits for them, and re-layouts  24 us
    reduce_sum x2, other arithmetic, kernel_terms(): jnp.sum(extended[first_row:first_row + length].astype(jnp.float32) * grad...  15.2 us
    convert_element_type x3, local copies, waits for them, and re-layouts, local(): member_delta.astype(jnp.bfloat16).reshape(length, inner_width)  14.6 us
    broadcast_in_dim x3, other arithmetic, local(): transpose_conv(grown, conv_kernel[member], length).astype(jnp.bfloat16)  13.8 us
    unnamed x3, other arithmetic  10.7 us
    ppermute x4, starting transfers between devices, shifted(): return lax.ppermute(value, axis, pairs)  9.71 us
    dot_general x1, matrix products, local(): jnp.einsum('nhts,nthv->nshv', probabilities, gradient_rows, preferred_ele...  9.56 us
  transfers between devices with their start and end apart: 5, of which 1 were waited for; matrix products, arithmetic and copies ran while one was open for 12% of the time, Pallas kernels for 0%

commit v1 on v0

v1 whole, which is shorter than its diff:
```python
import functools

import jax
import jax.numpy as jnp
from jax import lax
from jax.experimental import pallas as pl
from jax.experimental.pallas import tpu as pltpu
from jax.sharding import PartitionSpec as P

MESH = pl.DeviceIdType.MESH
BLK = 256
HALF = 128
LANES = 128
PAIR = 256
RIM = 16
CHUNK = 64
LOG2E = 1.4426950408889634
F32 = jnp.float32
BF16 = jnp.bfloat16
NT = (((1,), (1,)), ((), ()))
TN = (((0,), (0,)), ((), ()))
NN = (((1,), (0,)), ((), ()))


def dot(a, b, dims):
    return lax.dot_general(a, b, dims, preferred_element_type=F32)


def decay_tables(ld_ref, rows):
    upper = (
        lax.broadcasted_iota(jnp.int32, (BLK, BLK), 0)
        <= lax.broadcasted_iota(jnp.int32, (BLK, BLK), 1)
    ).astype(F32)
    heads, length = ld_ref.shape
    for b in range(length // BLK):
        span = slice(b * BLK, (b + 1) * BLK)
        sums = LOG2E * jnp.dot(
            ld_ref[:, span], upper, precision=lax.Precision.HIGHEST, preferred_element_type=F32
        )
        grown = jnp.exp2(sums)
        left = jnp.exp2(sums[:, BLK - 1 : BLK] - sums)
        for i in range(heads // 2):
            pair = slice(2 * i, 2 * i + 2)
            rows[i, :, span] = jnp.concatenate(
                [sums[pair], grown[pair], left[pair], jnp.zeros((2, BLK), F32)], axis=0
            )


def gradients_kernel(
    remote,
    q_any, k_any, v_any, q_ref, k_ref, v_ref, g_ref, ld_ref, w_ref,
    dq_ref, dk_ref, dv_ref, kg_ref,
    halo, xs, conv, scaled, rows, s_first, f_last, msg_out, msg_in,
    halo_send, halo_recv, msg_send, msg_recv,
):
    phase, i = pl.program_id(0), pl.program_id(1)
    steps = pl.num_programs(1)
    length = q_ref.shape[0]
    core = lax.axis_index("ctx") if remote else 0
    other = {"ctx": 1 - core}

    def halo_copy(m, source):
        return pltpu.make_async_remote_copy(
            src_ref=source.at[0, pl.ds(length - RIM, RIM), :],
            dst_ref=halo.at[m],
            send_sem=halo_send.at[m],
            recv_sem=halo_recv.at[m],
            device_id=other,
            device_id_type=MESH,
        )

    def state_copy(step):
        return pltpu.make_async_remote_copy(
            src_ref=msg_out.at[pl.ds(2 * step, 2)],
            dst_ref=msg_in.at[pl.ds(2 * step, 2)],
            send_sem=msg_send.at[step],
            recv_sem=msg_recv.at[step],
            device_id=other,
            device_id_type=MESH,
        )

    @pl.when((phase == 0) & (i == 0))
    def _():
        if remote:
            barrier = pltpu.get_barrier_semaphore()
            pl.semaphore_signal(barrier, inc=1, device_id=other, device_id_type=MESH)
            pl.semaphore_wait(barrier, 1)
            copies = [halo_copy(m, s) for m, s in enumerate((q_any, k_any, v_any))]
            for copy in copies:
                copy.start()
        decay_tables(ld_ref, rows)
        if remote:
            for copy in copies:
                copy.wait()
        else:
            halo[...] = jnp.zeros_like(halo)
            msg_in[...] = jnp.zeros_like(msg_in)

    @pl.when(phase == 0)
    def _():
        table = rows[i]
        columns = table.T
        for h in range(2):
            c = slice(h * LANES, (h + 1) * LANES)
            grown, left = columns[:, 2 + h : 3 + h], columns[:, 4 + h : 5 + h]
            for m, x_ref in enumerate((q_ref, k_ref, v_ref)):
                before = halo[m, :, pl.ds(pl.multiple_of(i * PAIR + h * LANES, LANES), LANES)]
                xs[i, h, m, 0:RIM] = jnp.where(core == 1, before.astype(F32), 0.0)
                for r in range(0, length, CHUNK):
                    xs[i, h, m, RIM + r : RIM + r + CHUNK] = x_ref[r : r + CHUNK, c].astype(F32)
                taps = [w_ref[m, j : j + 1, c] for j in range(4)]
                for r in range(0, length, CHUNK):
                    part = slice(r, r + CHUNK)
                    acc = taps[0] * xs[i, h, m, RIM + r : RIM + r + CHUNK]
                    for j in range(1, 4):
                        acc = acc + taps[j] * xs[i, h, m, RIM + r - j : RIM + r - j + CHUNK]
                    conv[m, i, part, c] = acc.astype(BF16)
                    if m > 0:
                        scaled[m, i, part, c] = (acc * left[part]).astype(BF16)
            for r in range(0, length, CHUNK):
                part = slice(r, r + CHUNK)
                scaled[0, i, part, c] = (g_ref[part, c].astype(F32) * grown[part]).astype(BF16)
            states, futures = [], []
            for b in range(2):
                part = slice(b * BLK, (b + 1) * BLK)
                states.append(dot(conv[1, i, part, c], scaled[2, i, part, c], TN))
                futures.append(dot(conv[0, i, part, c], scaled[0, i, part, c], TN))
            decay = [table[2 + h : 3 + h, (b + 1) * BLK - 1 : (b + 1) * BLK] for b in range(2)]
            s_first[2 * i + h] = states[0]
            f_last[2 * i + h] = futures[1]
            msg_out[2 * i + h] = jnp.where(
                core == 0, states[1] + decay[1] * states[0], futures[0] + decay[0] * futures[1]
            ).astype(BF16)
        if remote:
            state_copy(i).start()

    @pl.when(phase == 1)
    def _():
        if remote:
            state_copy(i).wait()
        table = rows[i]
        columns = table.T
        scale = 1.0 / LANES
        causal = lax.broadcasted_iota(jnp.int32, (HALF, HALF), 0) <= lax.broadcasted_iota(
            jnp.int32, (HALF, HALF), 1
        )
        for h in range(2):
            c = slice(h * LANES, (h + 1) * LANES)
            decay = [table[2 + h : 3 + h, (b + 1) * BLK - 1 : (b + 1) * BLK] for b in range(2)]
            message = msg_in[2 * i + h].astype(F32) * scale
            state_in = jnp.where(core == 1, message, 0.0)
            future_in = jnp.where(core == 0, message, 0.0)
            incoming = [state_in, decay[0] * state_in + scale * s_first[2 * i + h]]
            future = [decay[1] * future_in + scale * f_last[2 * i + h], future_in]
            kernel_sums = [[jnp.zeros((8, LANES), F32) for _ in range(4)] for _ in range(3)]
            for b in range(2):
                part = slice(b * BLK, (b + 1) * BLK)
                q, k, v = (conv[m, i, part, c] for m in range(3))
                wg, wk, wv = (scaled[m, i, part, c] for m in range(3))
                g = g_ref[part, c]
                before = incoming[b].astype(BF16)
                after = future[b].astype(BF16)
                row = table[h : h + 1, part] - 7.0
                column = columns[part, h : h + 1]

                def weight(s, t):
                    mine = jnp.exp2(
                        row[:, t * HALF : (t + 1) * HALF] - column[s * HALF : (s + 1) * HALF]
                    )
                    return jnp.where(causal, mine, 0.0) if s == t else mine

                top = jnp.concatenate([weight(0, 0), weight(0, 1)], axis=1)
                low = weight(1, 1)
                pt_top = (dot(k[:HALF], q, NT) * top).astype(BF16)
                pt_low = (dot(k[HALF:], q[HALF:], NT) * low).astype(BF16)
                gt_top = (dot(v[:HALF], g, NT) * top).astype(BF16)
                gt_low = (dot(v[HALF:], g[HALF:], NT) * low).astype(BF16)
                dk_far = dot(wv, after, NT)
                dv_far = dot(wk, after, NN)
                dq_far = dot(wg, before, NT)
                dk = [dot(gt_top, q, NN) + dk_far[:HALF], dot(gt_low, q[HALF:], NN) + dk_far[HALF:]]
                dv = [dot(pt_top, g, NN) + dv_far[:HALF], dot(pt_low, g[HALF:], NN) + dv_far[HALF:]]
                dq_near = dot(gt_top, k[:HALF], TN)
                dq = [
                    dq_near[:HALF] + dq_far[:HALF],
                    dq_near[HALF:] + dot(gt_low, k[HALF:], TN) + dq_far[HALF:],
                ]
                for m, (grads, ref) in enumerate(((dq, dq_ref), (dk, dk_ref), (dv, dv_ref))):
                    for half in range(2):
                        base = b * BLK + half * HALF
                        ref[base : base + HALF, c] = grads[half].astype(BF16)
                        for j in range(4):
                            shifted = xs[i, h, m, RIM + base - j : RIM + base - j + HALF]
                            terms = (shifted * grads[half]).reshape(HALF // 8, 8, LANES)
                            kernel_sums[m][j] = kernel_sums[m][j] + jnp.sum(terms, axis=0)
            kg_ref[:, c] = jnp.concatenate(
                [jnp.sum(kernel_sums[m][j], axis=0, keepdims=True) for m in range(3) for j in range(4)]
                + [jnp.zeros((4, LANES), F32)],
                axis=0,
            )


def gradients(query, key, value, out_grad, log_decay, conv_kernel, remote=True):
    _, length, width = query.shape
    heads = log_decay.shape[1]
    steps = width // PAIR
    first = lambda p, i: (0, 0, i * (1 - p) + (steps - 1) * p)
    both = lambda p, i: (0, 0, i)
    late = lambda p, i: (0, i * p)
    block = pl.BlockSpec((None, length, PAIR), first)
    out_block = pl.BlockSpec((length, PAIR), late)
    return pl.pallas_call(
        functools.partial(gradients_kernel, remote),
        grid=(2, steps),
        in_specs=[pl.BlockSpec(memory_space=pl.ANY)] * 3
        + [block] * 3
        + [
            pl.BlockSpec((None, length, PAIR), both),
            pl.BlockSpec((None, heads, length), lambda p, i: (0, 0, 0)),
            pl.BlockSpec((3, 4, PAIR), first),
        ],
        out_specs=[out_block] * 3 + [pl.BlockSpec((16, PAIR), late)],
        out_shape=[jax.ShapeDtypeStruct((length, width), BF16)] * 3
        + [jax.ShapeDtypeStruct((16, width), F32)],
        scratch_shapes=[
            pltpu.VMEM((3, RIM, width), BF16),
            pltpu.VMEM((steps, 2, 3, RIM + length, LANES), F32),
            pltpu.VMEM((3, steps, length, PAIR), BF16),
            pltpu.VMEM((3, steps, length, PAIR), BF16),
            pltpu.VMEM((steps, 8, length), F32),
            pltpu.VMEM((heads, LANES, LANES), F32),
            pltpu.VMEM((heads, LANES, LANES), F32),
            pltpu.VMEM((heads, LANES, LANES), BF16),
            pltpu.VMEM((heads, LANES, LANES), BF16),
            pltpu.SemaphoreType.DMA((3,)),
            pltpu.SemaphoreType.DMA((3,)),
            pltpu.SemaphoreType.DMA((steps,)),
            pltpu.SemaphoreType.DMA((steps,)),
        ],
        compiler_params=pltpu.CompilerParams(
            collective_id=0 if remote else None,
            has_side_effects=True,
            dimension_semantics=("arbitrary", "arbitrary"),
            vmem_limit_bytes=60 * 1024 * 1024,
        ),
        name="gradients",
    )(query, key, value, query, key, value, out_grad, log_decay, conv_kernel)


def reduce_kernel(
    dq_any, dk_any, dv_any, kg_ref,
    after_ref, out_ref,
    z_in, y_src, y_in, x_src, x_in,
    halo_send, halo_recv, z_send, z_recv, y_send, y_recv, x_send, x_recv,
):
    core, dp = lax.axis_index("ctx"), lax.axis_index("dp")
    z, y, x = dp // 16, lax.rem(dp // 4, 4), lax.rem(dp, 4)
    width = kg_ref.shape[1]
    z_width, y_width, x_width = width // 4, width // 16, width // 64

    def device(c, zz, yy, xx):
        return {"ctx": c, "dp": zz * 16 + yy * 4 + xx}

    def turned(value, by):
        return lax.rem(value + by, 4)

    z_peers = [(d, device(core, turned(z, d), y, x)) for d in range(1, 4)]
    y_peers = [(d, device(core, z, turned(y, d), x)) for d in range(1, 4)]
    x_peers = [
        (4 * e + d, device(core if e == 0 else 1 - core, z, y, turned(x, d)))
        for e in range(2)
        for d in range(4)
        if e + d > 0
    ]
    barrier = pltpu.get_barrier_semaphore()
    everyone = z_peers + y_peers + x_peers
    for _, peer in everyone:
        pl.semaphore_signal(barrier, inc=1, device_id=peer, device_id_type=MESH)
    pl.semaphore_wait(barrier, len(everyone))

    def send(source, target, send_sem, recv_sem, peer):
        copy = pltpu.make_async_remote_copy(
            src_ref=source, dst_ref=target, send_sem=send_sem, recv_sem=recv_sem,
            device_id=peer, device_id_type=MESH,
        )
        copy.start()
        return copy

    z_copies = [
        send(
            kg_ref.at[:, pl.ds(pl.multiple_of(turned(z, d) * z_width, LANES), z_width)],
            z_in.at[d - 1], z_send.at[d - 1], z_recv.at[d - 1], peer,
        )
        for d, peer in z_peers
    ]
    halo_copies = [
        send(
            source.at[pl.ds(0, RIM), :], after_ref.at[m], halo_send.at[m], halo_recv.at[m],
            device(1 - core, z, y, x),
        )
        for m, source in enumerate((dq_any, dk_any, dv_any))
    ]
    total = kg_ref[:, pl.ds(pl.multiple_of(z * z_width, LANES), z_width)]
    for d, copy in enumerate(z_copies):
        copy.wait()
        total = total + z_in[d]
    for p in range(4):
        y_src[p] = jnp.concatenate(
            [total[:, p * y_width : (p + 1) * y_width], jnp.zeros((16, 256 - y_width), F32)], axis=1
        )
    y_copies = [
        send(y_src.at[turned(y, d)], y_in.at[d - 1], y_send.at[d - 1], y_recv.at[d - 1], peer)
        for d, peer in y_peers
    ]
    total = y_src[y]
    for d, copy in enumerate(y_copies):
        copy.wait()
        total = total + y_in[d]
    for p in range(4):
        x_src[p] = jnp.concatenate(
            [total[:, p * x_width : (p + 1) * x_width], jnp.zeros((16, 128 - x_width), F32)], axis=1
        )
    x_copies = [
        send(x_src.at[turned(x, s % 4)], x_in.at[s - 1], x_send.at[s - 1], x_recv.at[s - 1], peer)
        for s, peer in x_peers
    ]
    total = x_src[x]
    for s, copy in enumerate(x_copies):
        copy.wait()
        total = total + x_in[s]
    total = total * (1.0 / 64)
    for m in range(3):
        out_ref[m] = total[4 * m : 4 * m + 4, :x_width]
    for copy in halo_copies:
        copy.wait()


def reduce_terms(dq, dk, dv, kg):
    width = dq.shape[1]
    dma = pltpu.SemaphoreType.DMA
    return pl.pallas_call(
        reduce_kernel,
        in_specs=[pl.BlockSpec(memory_space=pl.ANY)] * 3 + [pl.BlockSpec(memory_space=pltpu.VMEM)],
        out_specs=[pl.BlockSpec(memory_space=pltpu.VMEM)] * 2,
        out_shape=[
            jax.ShapeDtypeStruct((3, RIM, width), BF16),
            jax.ShapeDtypeStruct((3, 4, width // 64), F32),
        ],
        scratch_shapes=[
            pltpu.VMEM((3, 16, width // 4), F32),
            pltpu.VMEM((4, 16, 256), F32),
            pltpu.VMEM((3, 16, 256), F32),
            pltpu.VMEM((4, 16, 128), F32),
            pltpu.VMEM((7, 16, 128), F32),
            dma((3,)), dma((3,)), dma((3,)), dma((3,)), dma((3,)), dma((3,)), dma((7,)), dma((7,)),
        ],
        compiler_params=pltpu.CompilerParams(collective_id=1, has_side_effects=True),
        name="reduce_terms",
    )(dq, dk, dv, kg)


def spread_kernel(dq_ref, dk_ref, dv_ref, after_ref, w_ref, oq_ref, ok_ref, ov_ref, wide):
    core = lax.axis_index("ctx")
    length = dq_ref.shape[0]
    for m, (ref, out) in enumerate(((dq_ref, oq_ref), (dk_ref, ok_ref), (dv_ref, ov_ref))):
        for h in range(2):
            c = slice(h * LANES, (h + 1) * LANES)
            for r in range(0, length, CHUNK):
                wide[m, h, r : r + CHUNK] = ref[r : r + CHUNK, c].astype(F32)
            wide[m, h, length : length + RIM] = jnp.where(
                core == 0, after_ref[m, :, c].astype(F32), 0.0
            )
            taps = [w_ref[m, j : j + 1, c] for j in range(4)]
            for r in range(0, length, CHUNK):
                acc = taps[0] * wide[m, h, r : r + CHUNK]
                for j in range(1, 4):
                    acc = acc + taps[j] * wide[m, h, r + j : r + j + CHUNK]
                out[r : r + CHUNK, c] = acc.astype(BF16)


def spread(dq, dk, dv, after, conv_kernel):
    length, width = dq.shape
    column = lambda i: (0, i)
    return pl.pallas_call(
        spread_kernel,
        grid=(width // PAIR,),
        in_specs=[pl.BlockSpec((length, PAIR), column)] * 3
        + [
            pl.BlockSpec((3, RIM, PAIR), lambda i: (0, 0, i)),
            pl.BlockSpec((3, 4, PAIR), lambda i: (0, 0, i)),
        ],
        out_specs=[pl.BlockSpec((None, length, PAIR), lambda i: (0, 0, i))] * 3,
        out_shape=[jax.ShapeDtypeStruct((1, length, width), BF16)] * 3,
        scratch_shapes=[pltpu.VMEM((3, 2, length + RIM, LANES), F32)],
        compiler_params=pltpu.CompilerParams(dimension_semantics=("arbitrary",)),
        name="spread",
    )(dq, dk, dv, after, conv_kernel)


def local(query, key, value, out_grad, log_decay, conv_kernel):
    dq, dk, dv, kg = gradients(query, key, value, out_grad, log_decay, conv_kernel)
    after, kernel_grad = reduce_terms(dq, dk, dv, kg)
    outputs = spread(dq, dk, dv, after, conv_kernel)
    return (*outputs, kernel_grad)


def solution(mesh):
    rows = P("dp", "ctx", None)
    return jax.shard_map(
        local,
        mesh=mesh,
        in_specs=(rows, rows, rows, rows, P("dp", None, "ctx"), P()),
        out_specs=(rows, rows, rows, P(None, None, "dp")),
        check_vma=False,
    )
```

time: 296 us -> 73.8 us (0.25)
  waiting for transfers between devices: 128 us -> 0 us
  Pallas kernels: 0 us -> 71.9 us
  local copies, waits for them, and re-layouts: 57.1 us -> 0.6 us
  other arithmetic: 50.6 us -> 0 us
  matrix products: 35.3 us -> 0 us
  between operations: 14.6 us -> 0.66 us
  starting transfers between devices: 9.75 us -> 0 us
    psum x1 -> x0, waiting for transfers between devices: 128 us -> none  [local(): summed = lax.psum(kernel_sums, ('ctx', 'dp'))]
    pallas_call x0 -> x3, Pallas kernels: none -> 71.9 us  [the longest x1 38.7 us: gradients(): pl.pallas_call(functools.partial(gradients_kernel, remote), grid=(2, step...]
    dot_general x9 -> x0, matrix products: 35.3 us -> none  [the longest x1 9.56 us: local(): jnp.einsum('nhts,nthv->nshv', probabilities, gradient_rows, preferred_ele...]
    unnamed x73 -> x3, local copies, waits for them, and re-layouts: 24 us -> 0.6 us
    reduce_sum x2 -> x0, other arithmetic: 15.2 us -> none  [kernel_terms(): jnp.sum(extended[first_row:first_row + length].astype(jnp.float32) * grad...]
    convert_element_type x3 -> x0, local copies, waits for them, and re-layouts: 14.6 us -> none  [local(): member_delta.astype(jnp.bfloat16).reshape(length, inner_width)]
    broadcast_in_dim x3 -> x0, other arithmetic: 13.8 us -> none  [local(): transpose_conv(grown, conv_kernel[member], length).astype(jnp.bfloat16)]
    unnamed x3 -> x0, other arithmetic: 10.7 us -> none
  transfers between devices with their start and end apart: 5 -> 0, of which waited for: 1 -> 0; matrix products, arithmetic and copies ran while one was open for 12% -> 0% of each run, Pallas kernels for 0% -> 0%
where the time goes in v1:
time: 73.8 us; the launch traced here: 73.2 us
  Pallas kernels  71.9 us (97%)
    pallas_call x1, Pallas kernels, gradients(): pl.pallas_call(functools.partial(gradients_kernel, remote), grid=(2, step...  38.7 us
    pallas_call x1, Pallas kernels, reduce_terms(): pl.pallas_call(reduce_kernel, in_specs=[pl.BlockSpec(memory_space=pl.ANY)...  20.4 us
    pallas_call x1, Pallas kernels, spread(): pl.pallas_call(spread_kernel, grid=(width // PAIR,), in_specs=[pl.BlockSp...  12.8 us

profile of v1, /device:TPU:1, one launch (start us, length us, event | category | flops | bytes accessed | tf_op | source)
XLA Modules:
  0.0 73.2 jit_solution(777584173165053226)
XLA Ops:
  0.6 38.7 %gradients.1 = (bf16[512,3072]{1,0:T(8,128)(2,1)}, bf16[512,3072]{1,0:T(8,128)(2,1)}, bf16[512,3072]{1,0:T(8,128)(2,1)}, f32[16,3072]{1,0:T(8,128)}) custom-call(bf16[1,512,3072]{2,1,0:T(8,128)(2,1)} %q_ref.1, bf16[1,512,3072]{2,1,0:T(8,128)(2,1)} %k_ref.1, bf16[1,512,3072]{2,1,0:T(8,128)(2,1)} %v_ref.1, bf16[1,512,3072]{2,1,0:T(8,128)(2,1)} %q_ref.1, ...), custom_call_target="tpu_custom_call" | custom-call | tf_op jit(solution)/shard_map/gradients/pallas_call | solution.py:212
  39.3 20.4 %reduce_terms.1 = (bf16[3,16,3072]{2,1,0:T(8,128)(2,1)}, f32[3,4,48]{2,1,0:T(4,128)}) custom-call(bf16[512,3072]{1,0:T(8,128)(2,1)} %get-tuple-element.13.dq_any.dq_ref, bf16[512,3072]{1,0:T(8,128)(2,1)} %get-tuple-element.14.dk_any.dk_ref, bf16[512,3072]{1,0:T(8,128)(2,1)} %get-tuple-element.15.dv_any.dv_ref, f32[16,3072]{1,0:T(8,128)} %get-tuple-element.16.kg_ref), custom_call_target="tpu_custom_call" | custom-call | tf_op jit(solution)/shard_map/reduce_terms/pallas_call | solution.py:341
  59.8 0.0 copy-start
  59.8 12.8 %spread.1 = (bf16[1,512,3072]{2,1,0:T(8,128)(2,1)}, bf16[1,512,3072]{2,1,0:T(8,128)(2,1)}, bf16[1,512,3072]{2,1,0:T(8,128)(2,1)}) custom-call(bf16[512,3072]{1,0:T(8,128)(2,1)} %get-tuple-element.13.dq_any.dq_ref, bf16[512,3072]{1,0:T(8,128)(2,1)} %get-tuple-element.14.dk_any.dk_ref, bf16[512,3072]{1,0:T(8,128)(2,1)} %get-tuple-element.15.dv_any.dv_ref, ...), custom_call_target="tpu_custom_call" | custom-call | tf_op jit(solution)/shard_map/spread/pallas_call | solution.py:384
  72.6 0.0 copy-done
  72.6 0.6 copy.11
Async XLA Ops:
  59.8 12.8 %copy-start = (f32[3,4,48]{2,1,0:T(4,128)S(1)}, f32[3,4,48]{2,1,0:T(4,128)}, u32[]{:S(2)}) copy-start(f32[3,4,48]{2,1,0:T(4,128)} %get-tuple-element.29) | copy-start | bytes 6916

commit v2 on v0

v2 whole, which is shorter than its diff:
```python
import functools

import jax
import jax.numpy as jnp
from jax import lax
from jax.experimental import pallas as pl
from jax.experimental.pallas import tpu as pltpu
from jax.sharding import PartitionSpec as P

MESH = pl.DeviceIdType.MESH
BLK = 256
HALF = 128
LANES = 128
PAIR = 256
RIM = 16
CHUNK = 64
PIECES = ((0, 5), (5, 10), (10, 16))
LOG2E = 1.4426950408889634
F32 = jnp.float32
BF16 = jnp.bfloat16
NT = (((1,), (1,)), ((), ()))
TN = (((0,), (0,)), ((), ()))
NN = (((1,), (0,)), ((), ()))


def dot(a, b, dims):
    return lax.dot_general(a, b, dims, preferred_element_type=F32)


def decay_tables(ld_ref, rows):
    upper = (
        lax.broadcasted_iota(jnp.int32, (BLK, BLK), 0)
        <= lax.broadcasted_iota(jnp.int32, (BLK, BLK), 1)
    ).astype(F32)
    heads, length = ld_ref.shape
    for b in range(length // BLK):
        span = slice(b * BLK, (b + 1) * BLK)
        sums = LOG2E * jnp.dot(
            ld_ref[:, span], upper, precision=lax.Precision.HIGHEST, preferred_element_type=F32
        )
        grown = jnp.exp2(sums)
        left = jnp.exp2(sums[:, BLK - 1 : BLK] - sums)
        for i in range(heads // 2):
            pair = slice(2 * i, 2 * i + 2)
            rows[i, :, span] = jnp.concatenate(
                [sums[pair], grown[pair], left[pair], jnp.zeros((2, BLK), F32)], axis=0
            )


def down(row):
    return jnp.broadcast_to(row, (LANES, LANES)).T


def diagonal(a, b):
    zero = jnp.zeros_like(a)
    return jnp.concatenate(
        [jnp.concatenate([a, zero], axis=1), jnp.concatenate([zero, b], axis=1)], axis=0
    )


def rim_kernel(q_any, k_any, v_any, halo_any, send_sem, recv_sem):
    length = q_any.shape[1]
    other = {"ctx": 1 - lax.axis_index("ctx")}
    barrier = pltpu.get_barrier_semaphore()
    pl.semaphore_signal(barrier, inc=1, device_id=other, device_id_type=MESH)
    pl.semaphore_wait(barrier, 1)
    copies = [
        pltpu.make_async_remote_copy(
            src_ref=source.at[0, pl.ds(length - RIM, RIM), :],
            dst_ref=halo_any.at[m],
            send_sem=send_sem.at[m],
            recv_sem=recv_sem.at[m],
            device_id=other,
            device_id_type=MESH,
        )
        for m, source in enumerate((q_any, k_any, v_any))
    ]
    for copy in copies:
        copy.start()
    for copy in copies:
        copy.wait()


def rims(query, key, value):
    return pl.pallas_call(
        rim_kernel,
        in_specs=[pl.BlockSpec(memory_space=pl.ANY)] * 3,
        out_specs=pl.BlockSpec(memory_space=pl.ANY),
        out_shape=jax.ShapeDtypeStruct((3, RIM, query.shape[2]), BF16),
        scratch_shapes=[pltpu.SemaphoreType.DMA((3,)), pltpu.SemaphoreType.DMA((3,))],
        compiler_params=pltpu.CompilerParams(collective_id=0, has_side_effects=True),
        name="rims",
    )(query, key, value)


def main_kernel(
    remote,
    q_any, k_any, v_any, g_any, halo_ref, ld_ref, w_ref,
    oq_any, ok_any, ov_any, kernel_grad_ref,
    xs, store, scaled, rows, s_first, f_last, msg_out, msg_in,
    terms, pieces, landed, part_out, part_in,
    in_sem, out_sem, msg_send, msg_recv, rim_send, rim_recv, piece_send, piece_recv, part_send,
    part_recv,
):
    steps, _, length, _ = store.shape
    core = lax.axis_index("ctx") if remote else 0
    dp = lax.axis_index("dp") if remote else 0
    peers = pieces.shape[0]
    other = {"ctx": 1 - core}
    share = terms.shape[1] // peers

    def columns(i, h=0, width=PAIR):
        return pl.ds(pl.multiple_of(i * PAIR + h * LANES, LANES), width)

    def fetch(i, m):
        source = (q_any, k_any, v_any, g_any)[m]
        return pltpu.make_async_copy(source.at[0, :, columns(i)], store.at[i, m], in_sem.at[i, m])

    def flush(i, m):
        target = (oq_any, ok_any, ov_any)[m]
        return pltpu.make_async_copy(store.at[i, m], target.at[0, :, columns(i)], out_sem.at[i, m])

    def remote_copy(source, target, send_sem, recv_sem, device):
        return pltpu.make_async_remote_copy(
            src_ref=source, dst_ref=target, send_sem=send_sem, recv_sem=recv_sem,
            device_id=device, device_id_type=MESH,
        )

    def state_copy(i):
        pair = pl.ds(2 * i, 2)
        return remote_copy(msg_out.at[pair], msg_in.at[pair], msg_send.at[i], msg_recv.at[i], other)

    def rim_copy(i):
        return remote_copy(
            xs.at[i, :, :, pl.ds(RIM, 8), :], xs.at[i, :, :, pl.ds(RIM + length, 8), :],
            rim_send.at[i], rim_recv.at[i], other,
        )

    def loop(count, body):
        def step(i, carry):
            body(i)
            return carry

        lax.fori_loop(0, count, step, 0)

    @functools.partial(loop, steps)
    def _(i):
        for m in range(4):
            fetch(i, m).start()

    if remote:
        barrier = pltpu.get_barrier_semaphore()
        pl.semaphore_signal(barrier, inc=1, device_id=other, device_id_type=MESH)

        @functools.partial(loop, peers - 1)
        def _(d):
            peer = {"dp": lax.rem(dp + d + 1, peers)}
            pl.semaphore_signal(barrier, inc=1, device_id=peer, device_id_type=MESH)
    else:
        msg_in[...] = jnp.zeros_like(msg_in)

    decay_tables(ld_ref, rows)

    @functools.partial(loop, steps)
    def _(i):
        for m in range(4):
            fetch(i, m).wait()
        table = rows[i]
        for h in range(2):
            c = slice(h * LANES, (h + 1) * LANES)
            for m in range(3):
                before = halo_ref[m, :, columns(i, h, LANES)].astype(F32)
                xs[i, h, m, 0:RIM] = jnp.where(core == 1, before, 0.0)
                for r in range(0, length, CHUNK):
                    xs[i, h, m, RIM + r : RIM + r + CHUNK] = store[i, m, r : r + CHUNK, c].astype(F32)
            taps = [[w_ref[m, j : j + 1, columns(i, h, LANES)] for j in range(4)] for m in range(3)]
            for base in range(0, length, LANES):
                grown = down(table[2 + h : 3 + h, base : base + LANES])
                left = down(table[4 + h : 5 + h, base : base + LANES])
                for r in range(0, LANES, CHUNK):
                    part = slice(base + r, base + r + CHUNK)
                    near = slice(r, r + CHUNK)
                    for m in range(3):
                        at = RIM + base + r
                        acc = taps[m][0] * xs[i, h, m, at : at + CHUNK]
                        for j in range(1, 4):
                            acc = acc + taps[m][j] * xs[i, h, m, at - j : at - j + CHUNK]
                        store[i, m, part, c] = acc.astype(BF16)
                        if m > 0:
                            scaled[m, i, part, c] = (acc * left[near]).astype(BF16)
                    scaled[0, i, part, c] = (store[i, 3, part, c].astype(F32) * grown[near]).astype(BF16)
        first, last = pl.ds(0, BLK), pl.ds(BLK, BLK)
        own = pl.ds(pl.multiple_of((1 - core) * BLK, BLK), BLK)
        state = dot(store[i, 1, first, :], scaled[2, i, first, :], TN)
        future = dot(store[i, 0, last, :], scaled[0, i, last, :], TN)
        message = dot(store[i, 1 - core, own, :], scaled[2 - 2 * core, i, own, :], TN)
        for h in range(2):
            c = slice(h * LANES, (h + 1) * LANES)
            decay = [table[2 + h : 3 + h, (b + 1) * BLK - 1 : (b + 1) * BLK] for b in range(2)]
            s_first[2 * i + h] = state[c, c]
            f_last[2 * i + h] = future[c, c]
            msg_out[2 * i + h] = (
                message[c, c]
                + jnp.where(core == 0, decay[1] * state[c, c], decay[0] * future[c, c])
            ).astype(BF16)
        if remote:

            @pl.when(i == steps - 2)
            def _():
                pl.semaphore_wait(pltpu.get_barrier_semaphore(), peers)
                loop(steps - 1, lambda n: state_copy(n).start())

            @pl.when(i == steps - 1)
            def _():
                state_copy(steps - 1).start()

    @functools.partial(loop, steps)
    def _(i):
        if remote:
            state_copy(i).wait()
        table = rows[i]
        scale = 1.0 / LANES
        causal = lax.broadcasted_iota(jnp.int32, (HALF, HALF), 0) <= lax.broadcasted_iota(
            jnp.int32, (HALF, HALF), 1
        )
        blank = jnp.zeros((HALF, HALF), BF16)
        incoming, future = [], []
        for h in range(2):
            decay = [table[2 + h : 3 + h, (b + 1) * BLK - 1 : (b + 1) * BLK] for b in range(2)]
            message = msg_in[2 * i + h].astype(F32) * scale
            state_in = jnp.where(core == 1, message, 0.0)
            future_in = jnp.where(core == 0, message, 0.0)
            state = decay[0] * state_in + scale * s_first[2 * i + h]
            grads = decay[1] * future_in + scale * f_last[2 * i + h]
            incoming.append([state_in.astype(BF16), state.astype(BF16)])
            future.append([grads.astype(BF16), future_in.astype(BF16)])
        kernel_sums = [[[jnp.zeros((8, LANES), F32)] * 4 for _ in range(3)] for _ in range(2)]
        for b in (1, 0):
            part = slice(b * BLK, (b + 1) * BLK)
            for h in range(2):
                c = slice(h * LANES, (h + 1) * LANES)
                q, k, v, g = (store[i, m, part, c] for m in range(4))
                row = table[h : h + 1, part]

                def weight(s, t):
                    mine = jnp.exp2(
                        (row[:, t * HALF : (t + 1) * HALF] - 7.0)
                        - down(row[:, s * HALF : (s + 1) * HALF])
                    )
                    return jnp.where(causal, mine, 0.0) if s == t else mine

                top = jnp.concatenate([weight(0, 0), weight(0, 1)], axis=1)
                low = weight(1, 1)

                def masked(full):
                    upper = (full[:HALF] * top).astype(BF16)
                    lower = (full[HALF:, HALF:] * low).astype(BF16)
                    return jnp.concatenate(
                        [upper, jnp.concatenate([blank, lower], axis=1)], axis=0
                    )

                gt = masked(dot(v, g, NT))
                pt = masked(dot(k, q, NT))
                wg, wk, wv = (scaled[m, i, part, c] for m in range(3))
                before, after = incoming[h][b], future[h][b]
                grads = (
                    dot(gt, k, TN) + dot(wg, before, NT),
                    dot(gt, q, NN) + dot(wv, after, NT),
                    dot(pt, g, NN) + dot(wk, after, NN),
                )
                for m in range(3):
                    for half in (1, 0):
                        at = RIM + b * BLK + half * HALF
                        mine = grads[m][half * HALF : (half + 1) * HALF]
                        for j in range(4):
                            product = xs[i, h, m, at - j : at - j + HALF] * mine
                            kernel_sums[h][m][j] = kernel_sums[h][m][j] + jnp.sum(
                                product.reshape(HALF // 8, 8, LANES), axis=0
                            )
                        xs[i, h, m, at : at + HALF] = mine
        for h in range(2):
            sums = [
                jnp.sum(kernel_sums[h][m][j], axis=0, keepdims=True)
                for m in range(3)
                for j in range(4)
            ]
            terms[:, columns(i, h, LANES)] = jnp.concatenate(
                sums + [jnp.zeros((4, LANES), F32)], axis=0
            )
        if remote:
            rim_copy(i).start()
        span = 3 * PAIR
        start = (i // 3) * (span // share)
        for r, (low_piece, high_piece) in enumerate(PIECES):

            @pl.when(lax.rem(i, 3) == r)
            def _():
                block = terms[:, pl.ds(pl.multiple_of((i // 3) * span, LANES), span)]
                for p in range(low_piece, high_piece):
                    piece = block[:, p * share : (p + 1) * share]
                    wide = jnp.concatenate([piece, jnp.zeros((16, 64 - share), F32)], axis=1)
                    pieces[start + p] = jnp.concatenate([wide[:8], wide[8:]], axis=1)
                if remote:

                    @functools.partial(loop, high_piece - low_piece)
                    def _(p):
                        owner = start + low_piece + p

                        @pl.when(owner != dp)
                        def _():
                            slot = lax.rem(dp - owner + peers, peers)
                            remote_copy(
                                pieces.at[owner], landed.at[slot], piece_send, piece_recv,
                                {"dp": owner},
                            ).start()

    @functools.partial(loop, steps)
    def _(i):
        if remote:
            rim_copy(i).wait()
        for m in range(3):
            for h in range(2):
                c = slice(h * LANES, (h + 1) * LANES)
                tail = slice(RIM + length, RIM + length + 8)
                xs[i, h, m, tail] = jnp.where(core == 0, xs[i, h, m, tail], 0.0)
                taps = [w_ref[m, j : j + 1, columns(i, h, LANES)] for j in range(4)]
                for r in range(0, length, CHUNK):
                    at = RIM + r
                    acc = taps[0] * xs[i, h, m, at : at + CHUNK]
                    for j in range(1, 4):
                        acc = acc + taps[j] * xs[i, h, m, at + j : at + j + CHUNK]
                    store[i, m, r : r + CHUNK, c] = acc.astype(BF16)
        for m in range(3):
            flush(i, m).start()

    if remote:
        others = pl.ds(1, peers - 1)
        remote_copy(pieces.at[others], landed.at[others], piece_send, piece_recv, other).wait()
        total = pieces[dp] + jnp.sum(landed[1:], axis=0)
        part_out[...] = total
        copy = remote_copy(part_out, part_in, part_send, part_recv, other)
        copy.start()
        copy.wait()
        total = (total + part_in[...]) * (1.0 / peers)
    else:
        total = pieces[dp]
    kernel_grad_ref[0] = total[0:4, :share]
    kernel_grad_ref[1] = total[4:8, :share]
    kernel_grad_ref[2] = total[0:4, 64 : 64 + share]

    @functools.partial(loop, steps)
    def _(i):
        for m in range(3):
            flush(i, m).wait()


def gradients(query, key, value, out_grad, log_decay, conv_kernel, remote=True):
    _, length, width = query.shape
    heads = log_decay.shape[1]
    steps = width // PAIR
    peers = lax.axis_size("dp") if remote else 64
    dma = pltpu.SemaphoreType.DMA
    anywhere = pl.BlockSpec(memory_space=pl.ANY)
    vmem = pl.BlockSpec(memory_space=pltpu.VMEM)
    halo = rims(query, key, value) if remote else jnp.zeros((3, RIM, width), BF16)
    return pl.pallas_call(
        functools.partial(main_kernel, remote),
        in_specs=[anywhere] * 4 + [vmem] * 3,
        out_specs=[anywhere] * 3 + [vmem],
        out_shape=[jax.ShapeDtypeStruct((1, length, width), BF16)] * 3
        + [jax.ShapeDtypeStruct((3, 4, width // peers), F32)],
        scratch_shapes=[
            pltpu.VMEM((steps, 2, 3, RIM + length + 8, LANES), F32),
            pltpu.VMEM((steps, 4, length, PAIR), BF16),
            pltpu.VMEM((3, steps, length, PAIR), BF16),
            pltpu.VMEM((steps, 8, length), F32),
            pltpu.VMEM((heads, LANES, LANES), F32),
            pltpu.VMEM((heads, LANES, LANES), F32),
            pltpu.VMEM((heads, LANES, LANES), BF16),
            pltpu.VMEM((heads, LANES, LANES), BF16),
            pltpu.VMEM((16, width), F32),
            pltpu.VMEM((peers, 8, LANES), F32),
            pltpu.VMEM((peers, 8, LANES), F32),
            pltpu.VMEM((8, LANES), F32),
            pltpu.VMEM((8, LANES), F32),
            dma((steps, 4)), dma((steps, 3)),
            dma((steps,)), dma((steps,)), dma((steps,)), dma((steps,)),
            dma, dma, dma, dma,
        ],
        compiler_params=pltpu.CompilerParams(
            collective_id=1 if remote else None,
            has_side_effects=True,
            vmem_limit_bytes=60 * 1024 * 1024,
        ),
        name="gradients",
    )(query, key, value, out_grad, halo, log_decay[0], conv_kernel)


def local(query, key, value, out_grad, log_decay, conv_kernel):
    return tuple(gradients(query, key, value, out_grad, log_decay, conv_kernel))


def solution(mesh):
    rows = P("dp", "ctx", None)
    return jax.shard_map(
        local,
        mesh=mesh,
        in_specs=(rows, rows, rows, rows, P("dp", None, "ctx"), P()),
        out_specs=(rows, rows, rows, P(None, None, "dp")),
        check_vma=False,
    )
```

time: 296 us -> 57.3 us (0.19)
  waiting for transfers between devices: 128 us -> 0 us
  other arithmetic: 50.6 us -> 0 us
  local copies, waits for them, and re-layouts: 57.1 us -> 9.2 us
  Pallas kernels: 0 us -> 47.3 us
  matrix products: 35.3 us -> 0 us
  between operations: 14.6 us -> 0.66 us
  starting transfers between devices: 9.75 us -> 0 us
    psum x1 -> x0, waiting for transfers between devices: 128 us -> none  [local(): summed = lax.psum(kernel_sums, ('ctx', 'dp'))]
    pallas_call x0 -> x2, Pallas kernels: none -> 47.3 us  [the longest x1 44.2 us: gradients(): pl.pallas_call(functools.partial(main_kernel, remote), in_specs=[anywhere...]
    dot_general x9 -> x0, matrix products: 35.3 us -> none  [the longest x1 9.56 us: local(): jnp.einsum('nhts,nthv->nshv', probabilities, gradient_rows, preferred_ele...]
    reduce_sum x2 -> x0, other arithmetic: 15.2 us -> none  [kernel_terms(): jnp.sum(extended[first_row:first_row + length].astype(jnp.float32) * grad...]
    unnamed x73 -> x10, local copies, waits for them, and re-layouts: 24 us -> 9.2 us
    convert_element_type x3 -> x0, local copies, waits for them, and re-layouts: 14.6 us -> none  [local(): member_delta.astype(jnp.bfloat16).reshape(length, inner_width)]
    broadcast_in_dim x3 -> x0, other arithmetic: 13.8 us -> none  [local(): transpose_conv(grown, conv_kernel[member], length).astype(jnp.bfloat16)]
    unnamed x3 -> x0, other arithmetic: 10.7 us -> none
  transfers between devices with their start and end apart: 5 -> 0, of which waited for: 1 -> 0; matrix products, arithmetic and copies ran while one was open for 12% -> 0% of each run, Pallas kernels for 0% -> 0%
where the time goes in v2:
time: 57.3 us; the launch traced here: 57.2 us
  Pallas kernels  47.3 us (83%)
  local copies, waits for them, and re-layouts  9.2 us (16%)
  between operations  0.66 us (1%)
    pallas_call x1, Pallas kernels, gradients(): pl.pallas_call(functools.partial(main_kernel, remote), in_specs=[anywhere...  44.2 us
    unnamed x10, local copies, waits for them, and re-layouts  9.2 us
    pallas_call x1, Pallas kernels, rims(): pl.pallas_call(rim_kernel, in_specs=[pl.BlockSpec(memory_space=pl.ANY)] *...  3.11 us

profile of v2, /device:TPU:1, one launch (start us, length us, event | category | flops | bytes accessed | tf_op | source)
XLA Modules:
  0.0 57.2 jit_solution(6586575754364599216)
XLA Ops:
  0.6 3.1 %rims.1.halo_ref = bf16[3,16,3072]{2,1,0:T(8,128)(2,1)} custom-call(bf16[1,512,3072]{2,1,0:T(8,128)(2,1)} %q_any.3, bf16[1,512,3072]{2,1,0:T(8,128)(2,1)} %k_any.3, bf16[1,512,3072]{2,1,0:T(8,128)(2,1)} %v_any.3), custom_call_target="tpu_custom_call" | custom-call | tf_op jit(solution)/shard_map/rims/pallas_call | solution.py:85
  3.8 44.2 %gradients.1 = (bf16[1,512,3072]{2,1,0:T(8,128)(2,1)}, bf16[1,512,3072]{2,1,0:T(8,128)(2,1)}, bf16[1,512,3072]{2,1,0:T(8,128)(2,1)}, f32[3,4,48]{2,1,0:T(4,128)}) custom-call(bf16[1,512,3072]{2,1,0:T(8,128)(2,1)} %q_any.3, bf16[1,512,3072]{2,1,0:T(8,128)(2,1)} %k_any.3, bf16[1,512,3072]{2,1,0:T(8,128)(2,1)} %v_any.3, bf16[1,512,3072]{2,1,0:T(8,128)(2,1)} %g_any.1, ...), custom_call_target="tpu_custom_call" | custom-call | tf_op jit(solution)/shard_map/gradients/pallas_call | solution.py:366
  48.0 0.0 copy-start.1
  48.0 3.9 %copy.14 = bf16[1,512,3072]{2,1,0:T(8,128)(2,1)} copy(bf16[1,512,3072]{2,1,0:T(8,128)(2,1)} %get-tuple-element.8) | data formatting | bytes 6291456
  51.9 0.0 copy-done.1
  51.9 0.0 copy-start
  51.9 1.7 %copy.15 = bf16[1,512,3072]{2,1,0:T(8,128)(2,1)} copy(bf16[1,512,3072]{2,1,0:T(8,128)(2,1)S(1)} %copy-done.1) | data formatting | bytes 6291456
  53.6 1.4 %copy-done = bf16[1,512,3072]{2,1,0:T(8,128)(2,1)S(1)} copy-done((bf16[1,512,3072]{2,1,0:T(8,128)(2,1)S(1)}, bf16[1,512,3072]{2,1,0:T(8,128)(2,1)}, u32[]{:S(2)}) %copy-start) | copy-done | bytes 3145752
  54.9 0.0 copy-start.2
  54.9 1.7 %copy.16 = bf16[1,512,3072]{2,1,0:T(8,128)(2,1)} copy(bf16[1,512,3072]{2,1,0:T(8,128)(2,1)S(1)} %copy-done) | data formatting | bytes 6291456
  56.6 0.0 copy-done.2
  56.6 0.6 %copy.17 = f32[3,4,48]{2,1,0:T(4,128)} copy(f32[3,4,48]{2,1,0:T(4,128)S(1)} %copy-done.2) | data formatting | bytes 4608
Async XLA Ops:
  48.0 3.9 %copy-start.1 = (bf16[1,512,3072]{2,1,0:T(8,128)(2,1)S(1)}, bf16[1,512,3072]{2,1,0:T(8,128)(2,1)}, u32[]{:S(2)}) copy-start(bf16[1,512,3072]{2,1,0:T(8,128)(2,1)} %get-tuple-element.9) | copy-start | bytes 9437188
  51.9 3.0 %copy-start = (bf16[1,512,3072]{2,1,0:T(8,128)(2,1)S(1)}, bf16[1,512,3072]{2,1,0:T(8,128)(2,1)}, u32[]{:S(2)}) copy-start(bf16[1,512,3072]{2,1,0:T(8,128)(2,1)} %get-tuple-element.10) | copy-start | bytes 9437188
  54.9 1.7 %copy-start.2 = (f32[3,4,48]{2,1,0:T(4,128)S(1)}, f32[3,4,48]{2,1,0:T(4,128)}, u32[]{:S(2)}) copy-start(f32[3,4,48]{2,1,0:T(4,128)} %get-tuple-element.11) | copy-start | bytes 6916

commit v3 on v2

--- a/solution.py
+++ b/solution.py
@@ -85,21 +85,21 @@
     return pl.pallas_call(
         rim_kernel,
         in_specs=[pl.BlockSpec(memory_space=pl.ANY)] * 3,
-        out_specs=pl.BlockSpec(memory_space=pl.ANY),
-        out_shape=jax.ShapeDtypeStruct((3, RIM, query.shape[2]), BF16),
+        out_specs=pl.BlockSpec(memory_space=pltpu.VMEM),
+        out_shape=pltpu.VMEM((3, RIM, query.shape[2]), BF16),
         scratch_shapes=[pltpu.SemaphoreType.DMA((3,)), pltpu.SemaphoreType.DMA((3,))],
         compiler_params=pltpu.CompilerParams(collective_id=0, has_side_effects=True),
         name="rims",
-    )(query, key, value)
+    )(*(pltpu.with_memory_space_constraint(x, pltpu.HBM) for x in (query, key, value)))
 
 
 def main_kernel(
     remote,
     q_any, k_any, v_any, g_any, halo_ref, ld_ref, w_ref,
-    oq_any, ok_any, ov_any, kernel_grad_ref,
-    xs, store, scaled, rows, s_first, f_last, msg_out, msg_in,
+    store, kernel_grad_ref,
+    xs, scaled, rows, s_first, f_last, msg_out, msg_in,
     terms, pieces, landed, part_out, part_in,
-    in_sem, out_sem, msg_send, msg_recv, rim_send, rim_recv, piece_send, piece_recv, part_send,
+    in_sem, msg_send, msg_recv, rim_send, rim_recv, piece_send, piece_recv, part_send,
     part_recv,
 ):
     steps, _, length, _ = store.shape
@@ -116,10 +116,6 @@
         source = (q_any, k_any, v_any, g_any)[m]
         return pltpu.make_async_copy(source.at[0, :, columns(i)], store.at[i, m], in_sem.at[i, m])
 
-    def flush(i, m):
-        target = (oq_any, ok_any, ov_any)[m]
-        return pltpu.make_async_copy(store.at[i, m], target.at[0, :, columns(i)], out_sem.at[i, m])
-
     def remote_copy(source, target, send_sem, recv_sem, device):
         return pltpu.make_async_remote_copy(
             src_ref=source, dst_ref=target, send_sem=send_sem, recv_sem=recv_sem,
@@ -160,11 +156,48 @@
         msg_in[...] = jnp.zeros_like(msg_in)
 
     decay_tables(ld_ref, rows)
+    first, last = pl.ds(0, BLK), pl.ds(BLK, BLK)
+    own = pl.ds(pl.multiple_of((1 - core) * BLK, BLK), BLK)
+
+    def states(i):
+        table = rows[i]
+        state = dot(store[i, 1, first, :], scaled[2, i, first, :], TN)
+        future = dot(store[i, 0, last, :], scaled[0, i, last, :], TN)
+        message = dot(store[i, 1 - core, own, :], scaled[2 - 2 * core, i, own, :], TN)
+        for h in range(2):
+            c = slice(h * LANES, (h + 1) * LANES)
+            decay = [table[2 + h : 3 + h, (b + 1) * BLK - 1 : (b + 1) * BLK] for b in range(2)]
+            s_first[2 * i + h] = state[c, c]
+            f_last[2 * i + h] = future[c, c]
+            msg_out[2 * i + h] = (
+                message[c, c]
+                + jnp.where(core == 0, decay[1] * state[c, c], decay[0] * future[c, c])
+            ).astype(BF16)
+
+    def spread(i, h, low, high):
+        c = slice(h * LANES, (h + 1) * LANES)
+        for m in range(3):
+            taps = [w_ref[m, j : j + 1, columns(i, h, LANES)] for j in range(4)]
+            for r in range(low, high, CHUNK):
+                size = min(CHUNK, high - r)
+                at = RIM + r
+                acc = taps[0] * xs[i, h, m, at : at + size]
+                for j in range(1, 4):
+                    acc = acc + taps[j] * xs[i, h, m, at + j : at + j + size]
+                store[i, m, r : r + size, c] = acc.astype(BF16)
 
     @functools.partial(loop, steps)
     def _(i):
         for m in range(4):
             fetch(i, m).wait()
+        if remote:
+
+            @pl.when(i == steps - 1)
+            def _():
+                pl.semaphore_wait(pltpu.get_barrier_semaphore(), peers)
+                loop(steps - 2, lambda n: state_copy(n).start())
+
+        states(jnp.maximum(i - 1, 0))
         table = rows[i]
         for h in range(2):
             c = slice(h * LANES, (h + 1) * LANES)
@@ -189,30 +222,11 @@
                         if m > 0:
                             scaled[m, i, part, c] = (acc * left[near]).astype(BF16)
                     scaled[0, i, part, c] = (store[i, 3, part, c].astype(F32) * grown[near]).astype(BF16)
-        first, last = pl.ds(0, BLK), pl.ds(BLK, BLK)
-        own = pl.ds(pl.multiple_of((1 - core) * BLK, BLK), BLK)
-        state = dot(store[i, 1, first, :], scaled[2, i, first, :], TN)
-        future = dot(store[i, 0, last, :], scaled[0, i, last, :], TN)
-        message = dot(store[i, 1 - core, own, :], scaled[2 - 2 * core, i, own, :], TN)
-        for h in range(2):
-            c = slice(h * LANES, (h + 1) * LANES)
-            decay = [table[2 + h : 3 + h, (b + 1) * BLK - 1 : (b + 1) * BLK] for b in range(2)]
-            s_first[2 * i + h] = state[c, c]
-            f_last[2 * i + h] = future[c, c]
-            msg_out[2 * i + h] = (
-                message[c, c]
-                + jnp.where(core == 0, decay[1] * state[c, c], decay[0] * future[c, c])
-            ).astype(BF16)
-        if remote:
-
-            @pl.when(i == steps - 2)
-            def _():
-                pl.semaphore_wait(pltpu.get_barrier_semaphore(), peers)
-                loop(steps - 1, lambda n: state_copy(n).start())
-
-            @pl.when(i == steps - 1)
-            def _():
-                state_copy(steps - 1).start()
+
+    states(steps - 1)
+    if remote:
+        state_copy(steps - 2).start()
+        state_copy(steps - 1).start()
 
     @functools.partial(loop, steps)
     def _(i):
@@ -235,10 +249,10 @@
             incoming.append([state_in.astype(BF16), state.astype(BF16)])
             future.append([grads.astype(BF16), future_in.astype(BF16)])
         kernel_sums = [[[jnp.zeros((8, LANES), F32)] * 4 for _ in range(3)] for _ in range(2)]
-        for b in (1, 0):
-            part = slice(b * BLK, (b + 1) * BLK)
-            for h in range(2):
-                c = slice(h * LANES, (h + 1) * LANES)
+        for h in range(2):
+            c = slice(h * LANES, (h + 1) * LANES)
+            for b in (1, 0):
+                part = slice(b * BLK, (b + 1) * BLK)
                 q, k, v, g = (store[i, m, part, c] for m in range(4))
                 row = table[h : h + 1, part]
 
@@ -278,6 +292,8 @@
                                 product.reshape(HALF // 8, 8, LANES), axis=0
                             )
                         xs[i, h, m, at : at + HALF] = mine
+            if h == 0:
+                spread(i, h, 0, length - RIM)
         for h in range(2):
             sums = [
                 jnp.sum(kernel_sums[h][m][j], axis=0, keepdims=True)
@@ -318,20 +334,12 @@
     def _(i):
         if remote:
             rim_copy(i).wait()
-        for m in range(3):
-            for h in range(2):
-                c = slice(h * LANES, (h + 1) * LANES)
-                tail = slice(RIM + length, RIM + length + 8)
+        tail = slice(RIM + length, RIM + length + 8)
+        for h in range(2):
+            for m in range(3):
                 xs[i, h, m, tail] = jnp.where(core == 0, xs[i, h, m, tail], 0.0)
-                taps = [w_ref[m, j : j + 1, columns(i, h, LANES)] for j in range(4)]
-                for r in range(0, length, CHUNK):
-                    at = RIM + r
-                    acc = taps[0] * xs[i, h, m, at : at + CHUNK]
-                    for j in range(1, 4):
-                        acc = acc + taps[j] * xs[i, h, m, at + j : at + j + CHUNK]
-                    store[i, m, r : r + CHUNK, c] = acc.astype(BF16)
-        for m in range(3):
-            flush(i, m).start()
+        spread(i, 0, length - RIM, length)
+        spread(i, 1, 0, length)
 
     if remote:
         others = pl.ds(1, peers - 1)
@@ -348,11 +356,6 @@
     kernel_grad_ref[1] = total[4:8, :share]
     kernel_grad_ref[2] = total[0:4, 64 : 64 + share]
 
-    @functools.partial(loop, steps)
-    def _(i):
-        for m in range(3):
-            flush(i, m).wait()
-
 
 def gradients(query, key, value, out_grad, log_decay, conv_kernel, remote=True):
     _, length, width = query.shape
@@ -362,16 +365,20 @@
     dma = pltpu.SemaphoreType.DMA
     anywhere = pl.BlockSpec(memory_space=pl.ANY)
     vmem = pl.BlockSpec(memory_space=pltpu.VMEM)
-    halo = rims(query, key, value) if remote else jnp.zeros((3, RIM, width), BF16)
+    if remote:
+        halo = pltpu.with_memory_space_constraint(rims(query, key, value), pltpu.VMEM)
+    else:
+        halo = jnp.zeros((3, RIM, width), BF16)
     return pl.pallas_call(
         functools.partial(main_kernel, remote),
         in_specs=[anywhere] * 4 + [vmem] * 3,
-        out_specs=[anywhere] * 3 + [vmem],
-        out_shape=[jax.ShapeDtypeStruct((1, length, width), BF16)] * 3
-        + [jax.ShapeDtypeStruct((3, 4, width // peers), F32)],
+        out_specs=[vmem, vmem],
+        out_shape=[
+            pltpu.VMEM((steps, 4, length, PAIR), BF16),
+            pltpu.VMEM((3, 4, width // peers), F32),
+        ],
         scratch_shapes=[
             pltpu.VMEM((steps, 2, 3, RIM + length + 8, LANES), F32),
-            pltpu.VMEM((steps, 4, length, PAIR), BF16),
             pltpu.VMEM((3, steps, length, PAIR), BF16),
             pltpu.VMEM((steps, 8, length), F32),
             pltpu.VMEM((heads, LANES, LANES), F32),
@@ -383,21 +390,54 @@
             pltpu.VMEM((peers, 8, LANES), F32),
             pltpu.VMEM((8, LANES), F32),
             pltpu.VMEM((8, LANES), F32),
-            dma((steps, 4)), dma((steps, 3)),
+            dma((steps, 4)),
             dma((steps,)), dma((steps,)), dma((steps,)), dma((steps,)),
             dma, dma, dma, dma,
         ],
         compiler_params=pltpu.CompilerParams(
             collective_id=1 if remote else None,
             has_side_effects=True,
-            vmem_limit_bytes=60 * 1024 * 1024,
+            vmem_limit_bytes=46 * 1024 * 1024,
         ),
         name="gradients",
     )(query, key, value, out_grad, halo, log_decay[0], conv_kernel)
 
 
+def flush_kernel(store, kernel_grad_in, oq_any, ok_any, ov_any, kernel_grad_out, sem):
+    steps = store.shape[0]
+    copies = [
+        pltpu.make_async_copy(
+            store.at[i, m], out.at[0, :, pl.ds(i * PAIR, PAIR)], sem.at[i, m]
+        )
+        for i in range(steps)
+        for m, out in enumerate((oq_any, ok_any, ov_any))
+    ]
+    for copy in copies:
+        copy.start()
+    kernel_grad_out[...] = kernel_grad_in[...]
+    for copy in copies:
+        copy.wait()
+
+
+def flush(store, kernel_grad):
+    steps, _, length, _ = store.shape
+    anywhere = pl.BlockSpec(memory_space=pl.ANY)
+    vmem = pl.BlockSpec(memory_space=pltpu.VMEM)
+    return pl.pallas_call(
+        flush_kernel,
+        in_specs=[anywhere, vmem],
+        out_specs=[anywhere] * 3 + [vmem],
+        out_shape=[jax.ShapeDtypeStruct((1, length, steps * PAIR), BF16)] * 3
+        + [jax.ShapeDtypeStruct(kernel_grad.shape, F32)],
+        scratch_shapes=[pltpu.SemaphoreType.DMA((steps, 3))],
+        compiler_params=pltpu.CompilerParams(vmem_limit_bytes=16 * 1024 * 1024),
+        name="flush",
+    )(*(pltpu.with_memory_space_constraint(x, pltpu.VMEM) for x in (store, kernel_grad)))
+
+
 def local(query, key, value, out_grad, log_decay, conv_kernel):
-    return tuple(gradients(query, key, value, out_grad, log_decay, conv_kernel))
+    store, kernel_grad = gradients(query, key, value, out_grad, log_decay, conv_kernel)
+    return tuple(flush(store, kernel_grad))
 
 
 def solution(mesh):

time: 57.3 us -> 54.1 us (0.944)
  the two profiles are of different devices: /device:TPU:1 before, /device:TPU:121 now
where the time goes in v3:
time: 54.1 us; the launch traced here: 54 us
  Pallas kernels  53.4 us (99%)
  between operations  0.65 us (1%)
    pallas_call x1, Pallas kernels, gradients(): pl.pallas_call(functools.partial(main_kernel, remote), in_specs=[anywhere...  46.7 us
    pallas_call x1, Pallas kernels, flush(): pl.pallas_call(flush_kernel, in_specs=[anywhere, vmem], out_specs=[anywhe...  4.48 us
    pallas_call x1, Pallas kernels, rims(): pl.pallas_call(rim_kernel, in_specs=[pl.BlockSpec(memory_space=pl.ANY)] *...  2.24 us

profile of v3, /device:TPU:121, one launch (start us, length us, event | category | flops | bytes accessed | tf_op | source)
XLA Modules:
  0.0 54.0 jit_solution(16808896544676632577)
XLA Ops:
  0.6 2.2 %rims.1.halo_ref = bf16[3,16,3072]{2,1,0:T(8,128)(2,1)S(1)} custom-call(bf16[1,512,3072]{2,1,0:T(8,128)(2,1)} %q_any.3, bf16[1,512,3072]{2,1,0:T(8,128)(2,1)} %k_any.3, bf16[1,512,3072]{2,1,0:T(8,128)(2,1)} %v_any.3), custom_call_target="tpu_custom_call" | custom-call | tf_op jit(solution)/shard_map/rims/pallas_call | solution.py:85
  2.9 46.7 %gradients.1 = (bf16[12,4,512,256]{3,2,1,0:T(8,128)(2,1)S(1)}, f32[3,4,48]{2,1,0:T(4,128)S(1)}) custom-call(bf16[1,512,3072]{2,1,0:T(8,128)(2,1)} %q_any.3, bf16[1,512,3072]{2,1,0:T(8,128)(2,1)} %k_any.3, bf16[1,512,3072]{2,1,0:T(8,128)(2,1)} %v_any.3, bf16[1,512,3072]{2,1,0:T(8,128)(2,1)} %g_any.1, bf16[3,16,3072]{2,1,0:T(8,128)(2,1)S(1)} %rims.1.halo_ref, ...), custom_call_target="tpu_custom_call" | custom-call | tf_op jit(solution)/shard_map/gradients/pallas_call | solution.py:372
  49.5 4.5 %flush.1 = (bf16[1,512,3072]{2,1,0:T(8,128)(2,1)}, bf16[1,512,3072]{2,1,0:T(8,128)(2,1)}, bf16[1,512,3072]{2,1,0:T(8,128)(2,1)}, f32[3,4,48]{2,1,0:T(4,128)}) custom-call(bf16[12,4,512,256]{3,2,1,0:T(8,128)(2,1)S(1)} %get-tuple-element.6.store, f32[3,4,48]{2,1,0:T(4,128)S(1)} %get-tuple-element.7.kernel_grad_in), custom_call_target="tpu_custom_call" | custom-call | tf_op jit(solution)/shard_map/flush/pallas_call | solution.py:426

commit v4 on v3

--- a/solution.py
+++ b/solution.py
@@ -43,7 +43,7 @@
         for i in range(heads // 2):
             pair = slice(2 * i, 2 * i + 2)
             rows[i, :, span] = jnp.concatenate(
-                [sums[pair], grown[pair], left[pair], jnp.zeros((2, BLK), F32)], axis=0
+                [sums[pair], grown[pair], left[pair], sums[pair] - 7.0], axis=0
             )
 
 
@@ -58,46 +58,73 @@
     )
 
 
-def rim_kernel(q_any, k_any, v_any, halo_any, send_sem, recv_sem):
+def prepare_kernel(
+    remote, q_any, k_any, v_any, ld_any, w_any, halo, rows, taps, ld, send_sem, recv_sem, local_sem
+):
     length = q_any.shape[1]
-    other = {"ctx": 1 - lax.axis_index("ctx")}
-    barrier = pltpu.get_barrier_semaphore()
-    pl.semaphore_signal(barrier, inc=1, device_id=other, device_id_type=MESH)
-    pl.semaphore_wait(barrier, 1)
-    copies = [
-        pltpu.make_async_remote_copy(
-            src_ref=source.at[0, pl.ds(length - RIM, RIM), :],
-            dst_ref=halo_any.at[m],
-            send_sem=send_sem.at[m],
-            recv_sem=recv_sem.at[m],
-            device_id=other,
-            device_id_type=MESH,
-        )
-        for m, source in enumerate((q_any, k_any, v_any))
+    local = [
+        pltpu.make_async_copy(ld_any, ld, local_sem.at[0]),
+        pltpu.make_async_copy(w_any, taps, local_sem.at[1]),
     ]
+    for copy in local:
+        copy.start()
+    copies = []
+    if remote:
+        other = {"ctx": 1 - lax.axis_index("ctx")}
+        barrier = pltpu.get_barrier_semaphore()
+        pl.semaphore_signal(barrier, inc=1, device_id=other, device_id_type=MESH)
+        pl.semaphore_wait(barrier, 1)
+        copies = [
+            pltpu.make_async_remote_copy(
+                src_ref=source.at[0, pl.ds(length - RIM, RIM), :],
+                dst_ref=halo.at[m],
+                send_sem=send_sem.at[m],
+                recv_sem=recv_sem.at[m],
+                device_id=other,
+                device_id_type=MESH,
+            )
+            for m, source in enumerate((q_any, k_any, v_any))
+        ]
+    else:
+        halo[...] = jnp.zeros_like(halo)
     for copy in copies:
         copy.start()
+    local[0].wait()
+    decay_tables(ld, rows)
+    local[1].wait()
     for copy in copies:
         copy.wait()
 
 
-def rims(query, key, value):
+def prepare(query, key, value, log_decay, conv_kernel, remote):
+    _, length, width = query.shape
+    heads = log_decay.shape[0]
+    anywhere = pl.BlockSpec(memory_space=pl.ANY)
+    vmem = pl.BlockSpec(memory_space=pltpu.VMEM)
+    dma = pltpu.SemaphoreType.DMA
+    inputs = (query, key, value, log_decay, conv_kernel)
     return pl.pallas_call(
-        rim_kernel,
-        in_specs=[pl.BlockSpec(memory_space=pl.ANY)] * 3,
-        out_specs=pl.BlockSpec(memory_space=pltpu.VMEM),
-        out_shape=pltpu.VMEM((3, RIM, query.shape[2]), BF16),
-        scratch_shapes=[pltpu.SemaphoreType.DMA((3,)), pltpu.SemaphoreType.DMA((3,))],
-        compiler_params=pltpu.CompilerParams(collective_id=0, has_side_effects=True),
-        name="rims",
-    )(*(pltpu.with_memory_space_constraint(x, pltpu.HBM) for x in (query, key, value)))
+        functools.partial(prepare_kernel, remote),
+        in_specs=[anywhere] * 5,
+        out_specs=[vmem] * 3,
+        out_shape=[
+            pltpu.VMEM((3, RIM, width), BF16),
+            pltpu.VMEM((heads // 2, 8, length), F32),
+            pltpu.VMEM(conv_kernel.shape, F32),
+        ],
+        scratch_shapes=[pltpu.VMEM((heads, length), F32), dma((3,)), dma((3,)), dma((2,))],
+        compiler_params=pltpu.CompilerParams(
+            collective_id=0 if remote else None, has_side_effects=True
+        ),
+        name="prepare",
+    )(*(pltpu.with_memory_space_constraint(x, pltpu.HBM) for x in inputs))
 
 
 def main_kernel(
     remote,
-    q_any, k_any, v_any, g_any, halo_ref, ld_ref, w_ref,
+    q_any, k_any, v_any, g_any, halo_ref, rows, w_ref,
     store, kernel_grad_ref,
-    xs, scaled, rows, s_first, f_last, msg_out, msg_in,
+    xs, scaled, s_first, f_last, msg_out, msg_in, rim_out, rim_in,
     terms, pieces, landed, part_out, part_in,
     in_sem, msg_send, msg_recv, rim_send, rim_recv, piece_send, piece_recv, part_send,
     part_recv,
@@ -122,15 +149,18 @@
             device_id=device, device_id_type=MESH,
         )
 
-    def state_copy(i):
-        pair = pl.ds(2 * i, 2)
-        return remote_copy(msg_out.at[pair], msg_in.at[pair], msg_send.at[i], msg_recv.at[i], other)
-
-    def rim_copy(i):
-        return remote_copy(
-            xs.at[i, :, :, pl.ds(RIM, 8), :], xs.at[i, :, :, pl.ds(RIM + length, 8), :],
-            rim_send.at[i], rim_recv.at[i], other,
-        )
+    state_spans = ((0, 2), (2, steps - 2), (steps - 2, steps))
+    rim_spans = ((0, steps // 2), (steps // 2, steps))
+
+    def state_copy(n):
+        low, high = state_spans[n]
+        span = pl.ds(2 * low, 2 * (high - low))
+        return remote_copy(msg_out.at[span], msg_in.at[span], msg_send.at[n], msg_recv.at[n], other)
+
+    def rim_copy(n):
+        low, high = rim_spans[n]
+        span = pl.ds(low, high - low)
+        return remote_copy(rim_out.at[span], rim_in.at[span], rim_send.at[n], rim_recv.at[n], other)
 
     def loop(count, body):
         def step(i, carry):
@@ -155,15 +185,17 @@
     else:
         msg_in[...] = jnp.zeros_like(msg_in)
 
-    decay_tables(ld_ref, rows)
     first, last = pl.ds(0, BLK), pl.ds(BLK, BLK)
-    own = pl.ds(pl.multiple_of((1 - core) * BLK, BLK), BLK)
 
     def states(i):
         table = rows[i]
         state = dot(store[i, 1, first, :], scaled[2, i, first, :], TN)
         future = dot(store[i, 0, last, :], scaled[0, i, last, :], TN)
-        message = dot(store[i, 1 - core, own, :], scaled[2 - 2 * core, i, own, :], TN)
+        message = dot(
+            jnp.where(core == 0, store[i, 1, last, :], store[i, 0, first, :]),
+            jnp.where(core == 0, scaled[2, i, last, :], scaled[0, i, first, :]),
+            TN,
+        )
         for h in range(2):
             c = slice(h * LANES, (h + 1) * LANES)
             decay = [table[2 + h : 3 + h, (b + 1) * BLK - 1 : (b + 1) * BLK] for b in range(2)]
@@ -195,7 +227,8 @@
             @pl.when(i == steps - 1)
             def _():
                 pl.semaphore_wait(pltpu.get_barrier_semaphore(), peers)
-                loop(steps - 2, lambda n: state_copy(n).start())
+                state_copy(0).start()
+                state_copy(1).start()
 
         states(jnp.maximum(i - 1, 0))
         table = rows[i]
@@ -225,13 +258,17 @@
 
     states(steps - 1)
     if remote:
-        state_copy(steps - 2).start()
-        state_copy(steps - 1).start()
+        state_copy(2).start()
 
     @functools.partial(loop, steps)
     def _(i):
         if remote:
-            state_copy(i).wait()
+            for n, (low, _) in enumerate(state_spans):
+
+                @pl.when(i == low)
+                def _():
+                    state_copy(n).wait()
+
         table = rows[i]
         scale = 1.0 / LANES
         causal = lax.broadcasted_iota(jnp.int32, (HALF, HALF), 0) <= lax.broadcasted_iota(
@@ -255,10 +292,11 @@
                 part = slice(b * BLK, (b + 1) * BLK)
                 q, k, v, g = (store[i, m, part, c] for m in range(4))
                 row = table[h : h + 1, part]
+                lowered = table[6 + h : 7 + h, part]
 
                 def weight(s, t):
                     mine = jnp.exp2(
-                        (row[:, t * HALF : (t + 1) * HALF] - 7.0)
+                        lowered[:, t * HALF : (t + 1) * HALF]
                         - down(row[:, s * HALF : (s + 1) * HALF])
                     )
                     return jnp.where(causal, mine, 0.0) if s == t else mine
@@ -292,8 +330,6 @@
                                 product.reshape(HALF // 8, 8, LANES), axis=0
                             )
                         xs[i, h, m, at : at + HALF] = mine
-            if h == 0:
-                spread(i, h, 0, length - RIM)
         for h in range(2):
             sums = [
                 jnp.sum(kernel_sums[h][m][j], axis=0, keepdims=True)
@@ -303,8 +339,16 @@
             terms[:, columns(i, h, LANES)] = jnp.concatenate(
                 sums + [jnp.zeros((4, LANES), F32)], axis=0
             )
+        for h in range(2):
+            for m in range(3):
+                rim_out[i, h, m] = xs[i, h, m, RIM : RIM + 8]
         if remote:
-            rim_copy(i).start()
+            for n, (_, high) in enumerate(rim_spans):
+
+                @pl.when(i == high - 1)
+                def _():
+                    rim_copy(n).start()
+
         span = 3 * PAIR
         start = (i // 3) * (span // share)
         for r, (low_piece, high_piece) in enumerate(PIECES):
@@ -332,14 +376,20 @@
 
     @functools.partial(loop, steps)
     def _(i):
-        if remote:
-            rim_copy(i).wait()
+        spread(i, 0, 0, length - RIM)
+        spread(i, 1, 0, length - RIM)
+
+    if remote:
+        for n in range(len(rim_spans)):
+            rim_copy(n).wait()
+
+    @functools.partial(loop, steps)
+    def _(i):
         tail = slice(RIM + length, RIM + length + 8)
         for h in range(2):
             for m in range(3):
-                xs[i, h, m, tail] = jnp.where(core == 0, xs[i, h, m, tail], 0.0)
-        spread(i, 0, length - RIM, length)
-        spread(i, 1, 0, length)
+                xs[i, h, m, tail] = jnp.where(core == 0, rim_in[i, h, m], 0.0)
+            spread(i, h, length - RIM, length)
 
     if remote:
         others = pl.ds(1, peers - 1)
@@ -365,10 +415,8 @@
     dma = pltpu.SemaphoreType.DMA
     anywhere = pl.BlockSpec(memory_space=pl.ANY)
     vmem = pl.BlockSpec(memory_space=pltpu.VMEM)
-    if remote:
-        halo = pltpu.with_memory_space_constraint(rims(query, key, value), pltpu.VMEM)
-    else:
-        halo = jnp.zeros((3, RIM, width), BF16)
+    prepared = prepare(query, key, value, log_decay[0], conv_kernel, remote)
+    prepared = [pltpu.with_memory_space_constraint(x, pltpu.VMEM) for x in prepared]
     return pl.pallas_call(
         functools.partial(main_kernel, remote),
         in_specs=[anywhere] * 4 + [vmem] * 3,
@@ -380,18 +428,19 @@
         scratch_shapes=[
             pltpu.VMEM((steps, 2, 3, RIM + length + 8, LANES), F32),
             pltpu.VMEM((3, steps, length, PAIR), BF16),
-            pltpu.VMEM((steps, 8, length), F32),
             pltpu.VMEM((heads, LANES, LANES), F32),
             pltpu.VMEM((heads, LANES, LANES), F32),
             pltpu.VMEM((heads, LANES, LANES), BF16),
             pltpu.VMEM((heads, LANES, LANES), BF16),
+            pltpu.VMEM((steps, 2, 3, 8, LANES), F32),
+            pltpu.VMEM((steps, 2, 3, 8, LANES), F32),
             pltpu.VMEM((16, width), F32),
             pltpu.VMEM((peers, 8, LANES), F32),
             pltpu.VMEM((peers, 8, LANES), F32),
             pltpu.VMEM((8, LANES), F32),
             pltpu.VMEM((8, LANES), F32),
             dma((steps, 4)),
-            dma((steps,)), dma((steps,)), dma((steps,)), dma((steps,)),
+            dma((3,)), dma((3,)), dma((2,)), dma((2,)),
             dma, dma, dma, dma,
         ],
         compiler_params=pltpu.CompilerParams(
@@ -400,7 +449,10 @@
             vmem_limit_bytes=46 * 1024 * 1024,
         ),
         name="gradients",
-    )(query, key, value, out_grad, halo, log_decay[0], conv_kernel)
+    )(
+        *(pltpu.with_memory_space_constraint(x, pltpu.HBM) for x in (query, key, value, out_grad)),
+        *prepared,
+    )
 
 
 def flush_kernel(store, kernel_grad_in, oq_any, ok_any, ov_any, kernel_grad_out, sem):

time: 54.1 us -> 48.6 us (0.90)
  the two profiles are of different devices: /device:TPU:121 before, /device:TPU:1 now
where the time goes in v4:
time: 48.6 us; the launch traced here: 48.5 us
  Pallas kernels  47.9 us (99%)
  between operations  0.65 us (1%)
    pallas_call x1, Pallas kernels, gradients(): pl.pallas_call(functools.partial(main_kernel, remote), in_specs=[anywhere...  40.4 us
    pallas_call x1, Pallas kernels, flush(): pl.pallas_call(flush_kernel, in_specs=[anywhere, vmem], out_specs=[anywhe...  4.48 us
    pallas_call x1, Pallas kernels, prepare(): pl.pallas_call(functools.partial(prepare_kernel, remote), in_specs=[anywh...  3 us

profile of v4, /device:TPU:1, one launch (start us, length us, event | category | flops | bytes accessed | tf_op | source)
XLA Modules:
  0.0 48.5 jit_solution(3671322290614176358)
XLA Ops:
  0.6 3.0 %prepare.1 = (bf16[3,16,3072]{2,1,0:T(8,128)(2,1)S(1)}, f32[12,8,512]{2,1,0:T(8,128)S(1)}, f32[3,4,3072]{2,1,0:T(4,128)S(1)}) custom-call(bf16[1,512,3072]{2,1,0:T(8,128)(2,1)} %q_any.3, bf16[1,512,3072]{2,1,0:T(8,128)(2,1)} %k_any.3, bf16[1,512,3072]{2,1,0:T(8,128)(2,1)} %v_any.3, f32[24,512]{1,0:T(8,128)} %bitcast.1, f32[3,4,3072]{2,1,0:T(4,128)} %w_any.1), custom_call_target="tpu_custom_call" | custom-call | tf_op jit(solution)/shard_map/prepare/pallas_call | solution.py:106
  3.6 40.4 %gradients.1 = (bf16[12,4,512,256]{3,2,1,0:T(8,128)(2,1)S(1)}, f32[3,4,48]{2,1,0:T(4,128)S(1)}) custom-call(bf16[1,512,3072]{2,1,0:T(8,128)(2,1)} %q_any.3, bf16[1,512,3072]{2,1,0:T(8,128)(2,1)} %k_any.3, bf16[1,512,3072]{2,1,0:T(8,128)(2,1)} %v_any.3, bf16[1,512,3072]{2,1,0:T(8,128)(2,1)} %g_any.1, bf16[3,16,3072]{2,1,0:T(8,128)(2,1)S(1)} %get-tuple-element.9.halo_ref, ...), custom_call_target="tpu_custom_call" | custom-call | tf_op jit(solution)/shard_map/gradients/pallas_call | solution.py:420
  44.0 4.5 %flush.1 = (bf16[1,512,3072]{2,1,0:T(8,128)(2,1)}, bf16[1,512,3072]{2,1,0:T(8,128)(2,1)}, bf16[1,512,3072]{2,1,0:T(8,128)(2,1)}, f32[3,4,48]{2,1,0:T(4,128)}) custom-call(bf16[12,4,512,256]{3,2,1,0:T(8,128)(2,1)S(1)} %get-tuple-element.12.store, f32[3,4,48]{2,1,0:T(4,128)S(1)} %get-tuple-element.13.kernel_grad_in), custom_call_target="tpu_custom_call" | custom-call | tf_op jit(solution)/shard_map/flush/pallas_call | solution.py:478

commit v5 on v4

--- a/solution.py
+++ b/solution.py
@@ -14,7 +14,6 @@
 PAIR = 256
 RIM = 16
 CHUNK = 64
-PIECES = ((0, 5), (5, 10), (10, 16))
 LOG2E = 1.4426950408889634
 F32 = jnp.float32
 BF16 = jnp.bfloat16
@@ -134,7 +133,7 @@
     dp = lax.axis_index("dp") if remote else 0
     peers = pieces.shape[0]
     other = {"ctx": 1 - core}
-    share = terms.shape[1] // peers
+    share = (terms.shape[1] - LANES) // peers
 
     def columns(i, h=0, width=PAIR):
         return pl.ds(pl.multiple_of(i * PAIR + h * LANES, LANES), width)
@@ -205,6 +204,33 @@
                 message[c, c]
                 + jnp.where(core == 0, decay[1] * state[c, c], decay[0] * future[c, c])
             ).astype(BF16)
+
+    def first_piece(i):
+        return 16 * (i // 3) + 5 * lax.rem(i, 3)
+
+    def piece_count(i):
+        return jnp.where(lax.rem(i, 3) == 2, 6, 5)
+
+    def pack(i):
+        part = lax.rem(i, 3)
+        base = 3 * PAIR * (i // 3) + jnp.where(part == 0, 0, jnp.where(part == 1, 128, 384))
+        shift = jnp.where(part == 0, 0, jnp.where(part == 1, 512 - 112, 512 - 96))
+        window = pltpu.roll(terms[:, pl.ds(pl.multiple_of(base, LANES), 512)], shift, 1)
+        for n in range(6):
+            piece = window[:, n * share : n * share + 64]
+            pieces[first_piece(i) + n] = jnp.concatenate([piece[:8], piece[8:]], axis=1)
+
+    def send(i, count):
+        @functools.partial(loop, count)
+        def _(n):
+            owner = first_piece(i) + n
+
+            @pl.when(owner != dp)
+            def _():
+                slot = lax.rem(dp - owner + peers, peers)
+                remote_copy(
+                    pieces.at[owner], landed.at[slot], piece_send, piece_recv, {"dp": owner}
+                ).start()
 
     def spread(i, h, low, high):
         c = slice(h * LANES, (h + 1) * LANES)
@@ -230,10 +256,11 @@
                 state_copy(0).start()
                 state_copy(1).start()
 
-        states(jnp.maximum(i - 1, 0))
         table = rows[i]
         for h in range(2):
             c = slice(h * LANES, (h + 1) * LANES)
+            if h == 1:
+                states(jnp.maximum(i - 1, 0))
             for m in range(3):
                 before = halo_ref[m, :, columns(i, h, LANES)].astype(F32)
                 xs[i, h, m, 0:RIM] = jnp.where(core == 1, before, 0.0)
@@ -269,6 +296,7 @@
                 def _():
                     state_copy(n).wait()
 
+        pack(jnp.maximum(i - 1, 0))
         table = rows[i]
         scale = 1.0 / LANES
         causal = lax.broadcasted_iota(jnp.int32, (HALF, HALF), 0) <= lax.broadcasted_iota(
@@ -349,30 +377,12 @@
                 def _():
                     rim_copy(n).start()
 
-        span = 3 * PAIR
-        start = (i // 3) * (span // share)
-        for r, (low_piece, high_piece) in enumerate(PIECES):
-
-            @pl.when(lax.rem(i, 3) == r)
-            def _():
-                block = terms[:, pl.ds(pl.multiple_of((i // 3) * span, LANES), span)]
-                for p in range(low_piece, high_piece):
-                    piece = block[:, p * share : (p + 1) * share]
-                    wide = jnp.concatenate([piece, jnp.zeros((16, 64 - share), F32)], axis=1)
-                    pieces[start + p] = jnp.concatenate([wide[:8], wide[8:]], axis=1)
-                if remote:
-
-                    @functools.partial(loop, high_piece - low_piece)
-                    def _(p):
-                        owner = start + low_piece + p
-
-                        @pl.when(owner != dp)
-                        def _():
-                            slot = lax.rem(dp - owner + peers, peers)
-                            remote_copy(
-                                pieces.at[owner], landed.at[slot], piece_send, piece_recv,
-                                {"dp": owner},
-                            ).start()
+        if remote:
+            send(i - 1, jnp.where(i == 0, 0, piece_count(i - 1)))
+
+    pack(steps - 1)
+    if remote:
+        send(steps - 1, piece_count(steps - 1))
 
     @functools.partial(loop, steps)
     def _(i):
@@ -434,7 +444,7 @@
             pltpu.VMEM((heads, LANES, LANES), BF16),
             pltpu.VMEM((steps, 2, 3, 8, LANES), F32),
             pltpu.VMEM((steps, 2, 3, 8, LANES), F32),
-            pltpu.VMEM((16, width), F32),
+            pltpu.VMEM((16, width + LANES), F32),
             pltpu.VMEM((peers, 8, LANES), F32),
             pltpu.VMEM((peers, 8, LANES), F32),
             pltpu.VMEM((8, LANES), F32),
@@ -455,9 +465,9 @@
     )
 
 
-def flush_kernel(store, kernel_grad_in, oq_any, ok_any, ov_any, kernel_grad_out, sem):
+def flush_kernel(store, kernel_grad_in, oq_any, ok_any, ov_any, kernel_grad_out, sem, last_sem):
     steps = store.shape[0]
-    copies = [
+    copies = [pltpu.make_async_copy(kernel_grad_in, kernel_grad_out, last_sem)] + [
         pltpu.make_async_copy(
             store.at[i, m], out.at[0, :, pl.ds(i * PAIR, PAIR)], sem.at[i, m]
         )
@@ -466,7 +476,6 @@
     ]
     for copy in copies:
         copy.start()
-    kernel_grad_out[...] = kernel_grad_in[...]
     for copy in copies:
         copy.wait()
 
@@ -477,11 +486,11 @@
     vmem = pl.BlockSpec(memory_space=pltpu.VMEM)
     return pl.pallas_call(
         flush_kernel,
-        in_specs=[anywhere, vmem],
-        out_specs=[anywhere] * 3 + [vmem],
+        in_specs=[vmem, vmem],
+        out_specs=[anywhere] * 4,
         out_shape=[jax.ShapeDtypeStruct((1, length, steps * PAIR), BF16)] * 3
         + [jax.ShapeDtypeStruct(kernel_grad.shape, F32)],
-        scratch_shapes=[pltpu.SemaphoreType.DMA((steps, 3))],
+        scratch_shapes=[pltpu.SemaphoreType.DMA((steps, 3)), pltpu.SemaphoreType.DMA],
         compiler_params=pltpu.CompilerParams(vmem_limit_bytes=16 * 1024 * 1024),
         name="flush",
     )(*(pltpu.with_memory_space_constraint(x, pltpu.VMEM) for x in (store, kernel_grad)))

time: 48.6 us -> 47 us (0.967)
  Pallas kernels: 47.9 us -> 46.2 us
    pallas_call x1, Pallas kernels: 40.4 us -> 39.3 us  [gradients(): pl.pallas_call(functools.partial(main_kernel, remote), in_specs=[anywhere...]
    pallas_call x1, Pallas kernels: 4.48 us -> 3.9 us  [flush(): pl.pallas_call(flush_kernel, in_specs=[vmem, vmem], out_specs=[anywhere]...]
where the time goes in v5:
time: 47 us; the launch traced here: 46.8 us
  Pallas kernels  46.2 us (98%)
  between operations  0.65 us (1%)
    pallas_call x1, Pallas kernels, gradients(): pl.pallas_call(functools.partial(main_kernel, remote), in_specs=[anywhere...  39.3 us
    pallas_call x1, Pallas kernels, flush(): pl.pallas_call(flush_kernel, in_specs=[vmem, vmem], out_specs=[anywhere]...  3.9 us
    pallas_call x1, Pallas kernels, prepare(): pl.pallas_call(functools.partial(prepare_kernel, remote), in_specs=[anywh...  3 us

profile of v5, /device:TPU:1, one launch (start us, length us, event | category | flops | bytes accessed | tf_op | source)
XLA Modules:
  0.0 46.8 jit_solution(6073463538295917707)
XLA Ops:
  0.6 3.0 %prepare.1 = (bf16[3,16,3072]{2,1,0:T(8,128)(2,1)S(1)}, f32[12,8,512]{2,1,0:T(8,128)S(1)}, f32[3,4,3072]{2,1,0:T(4,128)S(1)}) custom-call(bf16[1,512,3072]{2,1,0:T(8,128)(2,1)} %q_any.3, bf16[1,512,3072]{2,1,0:T(8,128)(2,1)} %k_any.3, bf16[1,512,3072]{2,1,0:T(8,128)(2,1)} %v_any.3, f32[24,512]{1,0:T(8,128)} %bitcast.1, f32[3,4,3072]{2,1,0:T(4,128)} %w_any.1), custom_call_target="tpu_custom_call" | custom-call | tf_op jit(solution)/shard_map/prepare/pallas_call | solution.py:105
  3.6 39.3 %gradients.1 = (bf16[12,4,512,256]{3,2,1,0:T(8,128)(2,1)S(1)}, f32[3,4,48]{2,1,0:T(4,128)S(1)}) custom-call(bf16[1,512,3072]{2,1,0:T(8,128)(2,1)} %q_any.3, bf16[1,512,3072]{2,1,0:T(8,128)(2,1)} %k_any.3, bf16[1,512,3072]{2,1,0:T(8,128)(2,1)} %v_any.3, bf16[1,512,3072]{2,1,0:T(8,128)(2,1)} %g_any.1, bf16[3,16,3072]{2,1,0:T(8,128)(2,1)S(1)} %get-tuple-element.9.halo_ref, ...), custom_call_target="tpu_custom_call" | custom-call | tf_op jit(solution)/shard_map/gradients/pallas_call | solution.py:430
  42.9 3.9 %flush.1 = (bf16[1,512,3072]{2,1,0:T(8,128)(2,1)}, bf16[1,512,3072]{2,1,0:T(8,128)(2,1)}, bf16[1,512,3072]{2,1,0:T(8,128)(2,1)}, f32[3,4,48]{2,1,0:T(4,128)}) custom-call(bf16[12,4,512,256]{3,2,1,0:T(8,128)(2,1)S(1)} %get-tuple-element.12.store, f32[3,4,48]{2,1,0:T(4,128)S(1)} %get-tuple-element.13.kernel_grad_in), custom_call_target="tpu_custom_call" | custom-call | tf_op jit(solution)/shard_map/flush/pallas_call | solution.py:487

commit v6 on v5

--- a/solution.py
+++ b/solution.py
@@ -393,8 +393,7 @@
         for n in range(len(rim_spans)):
             rim_copy(n).wait()
 
-    @functools.partial(loop, steps)
-    def _(i):
+    for i in range(steps):
         tail = slice(RIM + length, RIM + length + 8)
         for h in range(2):
             for m in range(3):

time: 47 us -> 46.9 us (level)
  no operation moved by 1% of the time
where the time goes in v6:
time: 46.9 us; the launch traced here: 46.8 us
  Pallas kernels  46.1 us (98%)
  between operations  0.65 us (1%)
    pallas_call x1, Pallas kernels, gradients(): pl.pallas_call(functools.partial(main_kernel, remote), in_specs=[anywhere...  39.2 us
    pallas_call x1, Pallas kernels, flush(): pl.pallas_call(flush_kernel, in_specs=[vmem, vmem], out_specs=[anywhere]...  3.9 us
    pallas_call x1, Pallas kernels, prepare(): pl.pallas_call(functools.partial(prepare_kernel, remote), in_specs=[anywh...  3 us

profile of v6, /device:TPU:1, one launch (start us, length us, event | category | flops | bytes accessed | tf_op | source)
XLA Modules:
  0.0 46.8 jit_solution(10454062462911854569)
XLA Ops:
  0.6 3.0 %prepare.1 = (bf16[3,16,3072]{2,1,0:T(8,128)(2,1)S(1)}, f32[12,8,512]{2,1,0:T(8,128)S(1)}, f32[3,4,3072]{2,1,0:T(4,128)S(1)}) custom-call(bf16[1,512,3072]{2,1,0:T(8,128)(2,1)} %q_any.3, bf16[1,512,3072]{2,1,0:T(8,128)(2,1)} %k_any.3, bf16[1,512,3072]{2,1,0:T(8,128)(2,1)} %v_any.3, f32[24,512]{1,0:T(8,128)} %bitcast.1, f32[3,4,3072]{2,1,0:T(4,128)} %w_any.1), custom_call_target="tpu_custom_call" | custom-call | tf_op jit(solution)/shard_map/prepare/pallas_call | solution.py:105
  3.6 39.2 %gradients.1 = (bf16[12,4,512,256]{3,2,1,0:T(8,128)(2,1)S(1)}, f32[3,4,48]{2,1,0:T(4,128)S(1)}) custom-call(bf16[1,512,3072]{2,1,0:T(8,128)(2,1)} %q_any.3, bf16[1,512,3072]{2,1,0:T(8,128)(2,1)} %k_any.3, bf16[1,512,3072]{2,1,0:T(8,128)(2,1)} %v_any.3, bf16[1,512,3072]{2,1,0:T(8,128)(2,1)} %g_any.1, bf16[3,16,3072]{2,1,0:T(8,128)(2,1)S(1)} %get-tuple-element.9.halo_ref, ...), custom_call_target="tpu_custom_call" | custom-call | tf_op jit(solution)/shard_map/gradients/pallas_call | solution.py:429
  42.8 3.9 %flush.1 = (bf16[1,512,3072]{2,1,0:T(8,128)(2,1)}, bf16[1,512,3072]{2,1,0:T(8,128)(2,1)}, bf16[1,512,3072]{2,1,0:T(8,128)(2,1)}, f32[3,4,48]{2,1,0:T(4,128)}) custom-call(bf16[12,4,512,256]{3,2,1,0:T(8,128)(2,1)S(1)} %get-tuple-element.12.store, f32[3,4,48]{2,1,0:T(4,128)S(1)} %get-tuple-element.13.kernel_grad_in), custom_call_target="tpu_custom_call" | custom-call | tf_op jit(solution)/shard_map/flush/pallas_call | solution.py:486
